TPU v7x, 128 devices: a whole 4x4x4 slice. The times are simulated.
128 devices in a mesh: gx: 8 (over z, core), gy: 16 (over y, x).
Axes of the slice: x: 4, y: 4, z: 4, core: 2. Of those that a mesh axis runs over, the one named last changes fastest.
Arguments:
- old_state: bfloat16 [16384, 19, 128], P(('gx', 'gy')), may hold values from -6 to 6
- send_block: int32 [128, 768], P(('gx', 'gy')), may hold values from 0 to 127
- receive_slot_table: int32 [16384, 3], P(('gx', 'gy')), may hold values from 0 to 767, as said below
- interpolation_weight_tiles: bfloat16 [16384, 3, 128, 128], P(('gx', 'gy')), may hold values from -0.3125 to 0.3125
- velocity: float32 [3, 9, 128, 2048], P(None, None, 'gx', 'gy'), may hold values from -6 to 6
- node_mass: float32 [9, 128, 2048], P(None, 'gx', 'gy'), may hold values from 0.5 to 2
- spot_x: int32 [36], replicated, may hold values from 0 to 127
- spot_y: int32 [36], replicated, may hold values from 0 to 2047
Outputs:
- final_state: float32 [19, 8, 128, 2048], P(None, None, 'gx', 'gy')
- final_velocity: float32 [3, 9, 128, 2048], P(None, None, 'gx', 'gy')
Inputs may be any that keep to these rules, and one draw needn't show every extreme that they name: `receive_slot_table`: the 384 entries of one device's new blocks name distinct slots; so at most 6 of them come from one source device, and for every device some source device supplies exactly 6.
All inputs are finite; a program needn't handle non-finite values.
Results may differ from a plain program's by a relative error of at most 0.0003.
Values may be sent and summed in bfloat16 or wider, within the bound.
A program may use at most 64 MiB of HBM per device.

v0:
```python
import jax
import jax.numpy as jnp
from jax import lax
from jax.sharding import PartitionSpec as P

STEPS = 2


SHEAR = 1.0
BULK = 2.0
YIELD_STRESS = 2.0
HARD_ISO = 0.3
HARD_KIN = 0.5
TIME_STEP = 0.2
PEAK_PRESSURE = 1.5
RADIUS_SQUARED = 36.0


def passed_along(value, axis, steps):
    count = lax.axis_size(axis)
    initial, last = (max(0, -steps), min(count, count - steps))
    return lax.ppermute(value, axis, [(source, source + steps) for source in range(initial, last)])


def zsum(field):
    return field[:, :-1] + field[:, 1:]


def element_update(state, corner_00, corner_01, corner_10, corner_11):
    grad_x = 0.25 * zsum(corner_10 + corner_11 - corner_00 - corner_01)
    grad_y = 0.25 * zsum(corner_01 + corner_11 - corner_00 - corner_10)
    every = corner_00 + corner_01 + corner_10 + corner_11
    grad_z = 0.25 * (every[:, 1:] - every[:, :-1])
    strain = [
        TIME_STEP * grad_x[0],
        TIME_STEP * grad_y[1],
        TIME_STEP * grad_z[2],
        TIME_STEP * 0.5 * (grad_y[0] + grad_x[1]),
        TIME_STEP * 0.5 * (grad_z[1] + grad_y[2]),
        TIME_STEP * 0.5 * (grad_x[2] + grad_z[0]),
    ]
    trace = strain[0] + strain[1] + strain[2]
    lame = BULK - 2.0 * SHEAR / 3.0
    trial = []
    for index in range(6):
        value = state[index] + 2.0 * SHEAR * strain[index]
        if index < 3:
            value = value + lame * trace
        trial.append(value)
    mean_value = (trial[0] + trial[1] + trial[2]) / 3.0
    deviator = []
    for index in range(6):
        shifted = trial[index] - mean_value if index < 3 else trial[index]
        deviator.append(shifted - state[6 + index])
    norm_two = (
        deviator[0] ** 2
        + deviator[1] ** 2
        + deviator[2] ** 2
        + 2.0 * (deviator[3] ** 2 + deviator[4] ** 2 + deviator[5] ** 2)
    )
    equiv = jnp.sqrt(1.5 * norm_two)
    epbar = state[18]
    excess = jnp.maximum(equiv - (YIELD_STRESS + HARD_ISO * epbar), 0.0)
    dgamma = excess / (3.0 * SHEAR + HARD_ISO + HARD_KIN)
    factor = dgamma / jnp.maximum(equiv, YIELD_STRESS)
    stress = [trial[index] - 3.0 * SHEAR * factor * deviator[index] for index in range(6)]
    back = [state[6 + index] + HARD_KIN * factor * deviator[index] for index in range(6)]
    plastic = [state[12 + index] + 1.5 * factor * deviator[index] for index in range(6)]
    new_state = jnp.stack(stress + back + plastic + [epbar + dgamma])
    along_x = -0.25 * jnp.stack([stress[0], stress[3], stress[5]])
    along_y = -0.25 * jnp.stack([stress[3], stress[1], stress[4]])
    along_z = -0.25 * jnp.stack([stress[5], stress[4], stress[2]])
    zero_layer = jnp.zeros_like(along_z[:, :1])
    corner_forces = []
    for sign_a in (-1.0, 1.0):
        for sign_b in (-1.0, 1.0):
            sideways_neighbour = sign_a * along_x + sign_b * along_y
            lower = jnp.concatenate([sideways_neighbour - along_z, zero_layer], axis=1)
            upper = jnp.concatenate([zero_layer, sideways_neighbour + along_z], axis=1)
            corner_forces.append(lower + upper)
    return (new_state, corner_forces)


def velocity_corners(velocity):
    column = passed_along(velocity[..., :1], "gy", -1)
    right = jnp.concatenate([velocity[..., 1:], column], axis=3)
    paired = jnp.stack([velocity, right])
    row = passed_along(paired[:, :, :, :1, :], "gx", -1)
    ahead = jnp.concatenate([paired[:, :, :, 1:, :], row], axis=3)
    return (velocity, right, ahead[0], ahead[1])


def node_forces(corner_forces):
    lifted = jnp.stack([corner_forces[1], corner_forces[3]])
    rim_cols = passed_along(lifted[..., -1:], "gy", 1)
    moved = jnp.concatenate([rim_cols, lifted[..., :-1]], axis=4)
    closer_device = corner_forces[0] + moved[0]
    farther = corner_forces[2] + moved[1]
    rim_rows = passed_along(farther[:, :, -1:, :], "gx", 1)
    return closer_device + jnp.concatenate([rim_rows, farther[:, :, :-1, :]], axis=2)


def body(
    old_state,
    send_block,
    receive_slot_table,
    interpolation_weight_tiles,
    velocity,
    node_mass,
    spot_x,
    spot_y,
):
    comps = old_state.shape[1]
    width = old_state.shape[2]
    layers = velocity.shape[1] - 1
    length = velocity.shape[2]
    departing_blocks = old_state[send_block[0]]
    arrived = lax.all_to_all(
        departing_blocks, ("gx", "gy"), split_axis=0, concat_axis=0, tiled=True
    )
    picked_entries = arrived[receive_slot_table]
    remapped = jnp.einsum(
        "fylt,fyat->lfa",
        picked_entries,
        interpolation_weight_tiles,
        preferred_element_type=jnp.float32,
    )
    state = remapped.reshape(comps, layers, length, width)
    start_x = lax.axis_index("gx") * length
    start_y = lax.axis_index("gy") * width
    xs = (start_x + jnp.arange(length, dtype=jnp.int32)).astype(jnp.float32)
    ys = (start_y + jnp.arange(width, dtype=jnp.int32)).astype(jnp.float32)
    factor_x = jnp.exp(-((xs[None, :] - spot_x.astype(jnp.float32)[:, None]) ** 2) / RADIUS_SQUARED)
    factor_y = jnp.exp(-((ys[None, :] - spot_y.astype(jnp.float32)[:, None]) ** 2) / RADIUS_SQUARED)
    pressure = jnp.dot(factor_x.T, factor_y, precision=lax.Precision.HIGHEST)
    for step_index in range(STEPS):
        corner_00, corner_01, corner_10, corner_11 = velocity_corners(velocity)
        state, corner_forces = element_update(state, corner_00, corner_01, corner_10, corner_11)
        forces = node_forces(corner_forces)
        forces = forces.at[2, layers].add(-PEAK_PRESSURE * pressure)
        velocity = velocity + TIME_STEP * forces / node_mass[None]
    return (state, velocity)


def solution(mesh):
    return jax.shard_map(
        body,
        mesh=mesh,
        in_specs=(
            P(("gx", "gy"), None, None),
            P(("gx", "gy"), None),
            P(("gx", "gy"), None),
            P(("gx", "gy"), None, None, None),
            P(None, None, "gx", "gy"),
            P(None, "gx", "gy"),
            P(),
            P(),
        ),
        out_specs=(P(None, None, "gx", "gy"), P(None, None, "gx", "gy")),
        check_vma=False,
    )
```

profile of v0, /device:TPU:40, one launch (start us, length us, event | category | flops | bytes accessed | tf_op | source)
XLA Modules:
  0.0 170.2 jit_solution(15283377505927026816)
XLA Ops:
  0.6 0.0 copy-start
  0.6 0.8 fusion.68
  1.4 0.3 copy-done
  1.7 17.2 %gather_fusion = bf16[768,19,128]{2,0,1:T(8,128)(2,1)} fusion(bf16[128,19,128]{2,0,1:T(8,128)(2,1)S(1)} %copy-done, s32[1024]{0:T(1024)S(1)} %pad_clamp_fusion.1), kind=kCustom, calls=%fused_computation | custom fusion | bytes 7474176 | tf_op jit(solution)/shard_map/gather | solution.py:117
  18.9 6.7 %copy.19 = bf16[768,19,128]{2,1,0:T(8,128)(2,1)} copy(bf16[768,19,128]{2,0,1:T(8,128)(2,1)} %gather_fusion) | data formatting | bytes 7471104 | tf_op jit(solution)/shard_map/gather | solution.py:117
  25.6 10.6 %all-to-all-start = ((bf16[768,19,128]{2,1,0:T(8,128)(2,1)}), bf16[768,19,128]{2,1,0:T(8,128)(2,1)}, u32[]{:S(2)}, u32[]{:S(2)}) async-start(bf16[768,19,128]{2,1,0:T(8,128)(2,1)} %copy.19), calls=%async_computation | async-start | bytes 9437184 | tf_op jit(solution)/shard_map/all_to_all | solution.py:118
  36.2 4.6 %collective-permute-start = (f32[3,9,16,1]{3,2,1,0:T(8,128)S(1)}, f32[3,9,16,1]{3,2,1,0:T(8,128)S(1)}, u32[]{:S(2)}, u32[]{:S(2)}) collective-permute-start(f32[3,9,16,1]{3,2,1,0:T(8,128)S(1)} %bitcast.95), channel_id=1, source_target_pairs={{1,0},{2,1},{3,2},{4,3},{5,4},{6,5},{7,6},{8,7},{9,8},{10,9},{11,1... | collective-permute-start | bytes 5192 | tf_op jit(solution)/shard_map/ppermute | solution.py:22
  40.8 0.1 copy.20
  41.0 0.2 reshape.510
  41.2 0.1 slice.305
  41.3 51.8 %collective-permute-done = f32[3,9,16,1]{3,2,1,0:T(8,128)S(1)} collective-permute-done((f32[3,9,16,1]{3,2,1,0:T(8,128)S(1)}, f32[3,9,16,1]{3,2,1,0:T(8,128)S(1)}, u32[]{:S(2)}, u32[]{:S(2)}) %collective-permute-start) | collective-permute-done | bytes 1760 | tf_op jit(solution)/shard_map/ppermute | solution.py:22
  93.1 0.1 fusion.83
  93.2 2.1 %collective-permute-start.1 = (f32[2,3,9,1,128]{4,3,2,1,0:T(1,128)S(1)}, f32[2,3,9,1,128]{4,3,2,1,0:T(1,128)S(1)}, u32[]{:S(2)}, u32[]{:S(2)}) collective-permute-start(f32[2,3,9,1,128]{4,3,2,1,0:T(1,128)S(1)} %pad_maximum_fusion.11), channel_id=1, source_target_pairs={{16,0},{32,16},{48,32},{64,48},{80,64},{96,80},{112,96},{17,1},{33... | collective-permute-start | bytes 82952 | tf_op jit(solution)/shard_map/ppermute | solution.py:22
  95.4 1.3 collective-permute-done.1
  96.7 0.1 subtract_subtract_fusion.3
  96.8 0.7 fusion.20
  97.5 0.1 subtract_subtract_fusion.2
  97.7 0.7 fusion.18
  98.4 0.0 all-to-all-done
  98.4 3.6 %gather_fusion.1 = bf16[384,19,128]{2,1,0:T(8,128)(2,1)S(1)} fusion(bf16[768,19,128]{2,1,0:T(8,128)(2,1)} %all-to-all-done, s32[1024]{0:T(1024)S(1)} %pad_clamp_fusion), kind=kCustom, calls=%fused_computation.1 | custom fusion | bytes 3737088 | tf_op jit(solution)/shard_map/gather | solution.py:121
  102.0 7.4 %convolution_bitcast_fusion = f32[19,128,128]{2,0,1:T(8,128)S(1)} fusion(bf16[128,3,19,128]{3,2,1,0:T(8,128)(2,1)S(1)} %bitcast.94, bf16[128,3,128,128]{3,2,1,0:T(8,128)(2,1)} %param.15), kind=kOutput, calls=%fused_computation.2 | convolution fusion | flops 239075328 | bytes 15695872 | tf_op jit(solution)/shard_map/fylt,fyat->lfa/dot_general | solution.py:122
  109.4 1.0 fusion.81
  110.4 0.0 copy-done.2
  110.4 0.0 copy-done.3
  110.5 0.2 multiply_subtract_fusion.6
  110.6 0.1 multiply_subtract_fusion.9
  110.7 0.1 fusion.37
  110.8 0.1 fusion.35
  110.8 0.1 fusion.40
  111.0 0.2 slice_maximum_fusion.2
  111.1 3.8 %collective-permute-start.2 = (f32[2,3,9,16,1]{4,3,2,1,0:T(8,128)S(1)}, f32[2,3,9,16,1]{4,3,2,1,0:T(8,128)S(1)}, u32[]{:S(2)}, u32[]{:S(2)}) collective-permute-start(f32[2,3,9,16,1]{4,3,2,1,0:T(8,128)S(1)} %slice_maximum_fusion.2), channel_id=1, source_target_pairs={{0,1},{1,2},{2,3},{3,4},{4,5},{5,6},{6,7},{7,8},{8,9},{9,10},{10,1... | collective-permute-start | bytes 10376 | tf_op jit(solution)/shard_map/ppermute | solution.py:22
  115.0 0.1 fusion.34
  115.0 0.0 copy-start.7
  115.1 0.0 copy-start.8
  115.1 12.3 %collective-permute-done.2 = f32[2,3,9,16,1]{4,3,2,1,0:T(8,128)S(1)} collective-permute-done((f32[2,3,9,16,1]{4,3,2,1,0:T(8,128)S(1)}, f32[2,3,9,16,1]{4,3,2,1,0:T(8,128)S(1)}, u32[]{:S(2)}, u32[]{:S(2)}) %collective-permute-start.2) | collective-permute-done | bytes 3488 | tf_op jit(solution)/shard_map/ppermute | solution.py:22
  127.3 0.2 fusion.2
  127.5 0.0 copy-start.4
  127.6 2.6 %collective-permute-start.3 = (f32[3,9,1,128]{3,2,1,0:T(1,128)S(1)}, f32[3,9,1,128]{3,2,1,0:T(1,128)S(1)}, u32[]{:S(2)}, u32[]{:S(2)}) collective-permute-start(f32[3,9,1,128]{3,2,1,0:T(1,128)S(1)} %slice.419), channel_id=1, source_target_pairs={{0,16},{16,32},{32,48},{48,64},{64,80},{80,96},{96,112},{1,17},{17... | collective-permute-start | bytes 41480 | tf_op jit(solution)/shard_map/ppermute | solution.py:22
  130.2 2.4 %collective-permute-done.3 = f32[3,9,1,128]{3,2,1,0:T(1,128)S(1)} collective-permute-done((f32[3,9,1,128]{3,2,1,0:T(1,128)S(1)}, f32[3,9,1,128]{3,2,1,0:T(1,128)S(1)}, u32[]{:S(2)}, u32[]{:S(2)}) %collective-permute-start.3) | collective-permute-done | bytes 13856 | tf_op jit(solution)/shard_map/ppermute | solution.py:22
  132.6 0.1 fusion.13
  132.7 0.2 fusion.59
  132.9 0.0 copy-done.4
  133.0 2.4 %collective-permute-start.4 = (f32[3,9,16,1]{3,2,1,0:T(8,128)S(1)}, f32[3,9,16,1]{3,2,1,0:T(8,128)S(1)}, u32[]{:S(2)}, u32[]{:S(2)}) collective-permute-start(f32[3,9,16,1]{3,2,1,0:T(8,128)S(1)} %bitcast.91), channel_id=1, source_target_pairs={{1,0},{2,1},{3,2},{4,3},{5,4},{6,5},{7,6},{8,7},{9,8},{10,9},{11,1... | collective-permute-start | bytes 5192 | tf_op jit(solution)/shard_map/ppermute | solution.py:22
  135.4 0.1 slice.422
  135.5 6.6 %collective-permute-done.4 = f32[3,9,16,1]{3,2,1,0:T(8,128)S(1)} collective-permute-done((f32[3,9,16,1]{3,2,1,0:T(8,128)S(1)}, f32[3,9,16,1]{3,2,1,0:T(8,128)S(1)}, u32[]{:S(2)}, u32[]{:S(2)}) %collective-permute-start.4) | collective-permute-done | bytes 1760 | tf_op jit(solution)/shard_map/ppermute | solution.py:22
  142.1 0.1 fusion.82
  142.3 1.9 %collective-permute-start.5 = (f32[2,3,9,1,128]{4,3,2,1,0:T(1,128)S(1)}, f32[2,3,9,1,128]{4,3,2,1,0:T(1,128)S(1)}, u32[]{:S(2)}, u32[]{:S(2)}) collective-permute-start(f32[2,3,9,1,128]{4,3,2,1,0:T(1,128)S(1)} %pad_maximum_fusion.10), channel_id=1, source_target_pairs={{16,0},{32,16},{48,32},{64,48},{80,64},{96,80},{112,96},{17,1},{33... | collective-permute-start | bytes 82952 | tf_op jit(solution)/shard_map/ppermute | solution.py:22
  144.2 1.5 collective-permute-done.5
  145.7 0.1 subtract_subtract_fusion.1
  145.9 0.1 subtract_subtract_fusion
  146.1 0.2 constant_dynamic-update-slice_fusion.5
  146.5 0.1 fusion.48
  146.5 0.1 fusion.45
  146.6 0.1 fusion.42
  146.9 0.2 slice_maximum_fusion
  147.1 1.9 %collective-permute-start.6 = (f32[2,3,9,16,1]{4,3,2,1,0:T(8,128)S(1)}, f32[2,3,9,16,1]{4,3,2,1,0:T(8,128)S(1)}, u32[]{:S(2)}, u32[]{:S(2)}) collective-permute-start(f32[2,3,9,16,1]{4,3,2,1,0:T(8,128)S(1)} %slice_maximum_fusion), channel_id=1, source_target_pairs={{0,1},{1,2},{2,3},{3,4},{4,5},{5,6},{6,7},{7,8},{8,9},{9,10},{10,1... | collective-permute-start | bytes 10376 | tf_op jit(solution)/shard_map/ppermute | solution.py:22
  149.2 0.1 fusion.43
  149.3 14.8 %collective-permute-done.6 = f32[2,3,9,16,1]{4,3,2,1,0:T(8,128)S(1)} collective-permute-done((f32[2,3,9,16,1]{4,3,2,1,0:T(8,128)S(1)}, f32[2,3,9,16,1]{4,3,2,1,0:T(8,128)S(1)}, u32[]{:S(2)}, u32[]{:S(2)}) %collective-permute-start.6) | collective-permute-done | bytes 3488 | tf_op jit(solution)/shard_map/ppermute | solution.py:22
  164.1 0.2 fusion.1
  164.3 1.9 %collective-permute-start.7 = (f32[3,9,1,128]{3,2,1,0:T(1,128)S(1)}, f32[3,9,1,128]{3,2,1,0:T(1,128)S(1)}, u32[]{:S(2)}, u32[]{:S(2)}) collective-permute-start(f32[3,9,1,128]{3,2,1,0:T(1,128)S(1)} %slice.453), channel_id=1, source_target_pairs={{0,16},{16,32},{32,48},{48,64},{64,80},{80,96},{96,112},{1,17},{17... | collective-permute-start | bytes 41480 | tf_op jit(solution)/shard_map/ppermute | solution.py:22
  166.3 0.0 copy-start.5
  166.3 3.0 %collective-permute-done.7 = f32[3,9,1,128]{3,2,1,0:T(1,128)S(1)} collective-permute-done((f32[3,9,1,128]{3,2,1,0:T(1,128)S(1)}, f32[3,9,1,128]{3,2,1,0:T(1,128)S(1)}, u32[]{:S(2)}, u32[]{:S(2)}) %collective-permute-start.7) | collective-permute-done | bytes 13856 | tf_op jit(solution)/shard_map/ppermute | solution.py:22
  169.4 0.1 fusion.9
  169.4 0.7 divide_add_fusion
  (53 shorter events, 1.1 us)
Async XLA Ops:
  0.6 1.1 copy-start
  25.6 10.6 %copy-start.1 = (f32[3,9,16,128]{3,2,1,0:T(8,128)S(1)}, f32[3,9,16,128]{3,2,1,0:T(8,128)}, u32[]{:S(2)}) copy-start(f32[3,9,16,128]{3,2,1,0:T(8,128)} %param.16) | copy-start | bytes 663556
  25.6 15.2 %copy-start.6 = (s32[128,3]{0,1:T(4,128)S(1)}, s32[128,3]{0,1:T(4,128)}, u32[]{:S(2)}) copy-start(s32[128,3]{0,1:T(4,128)} %param.14) | copy-start | bytes 4612
  25.6 72.8 %all-to-all-start = ((bf16[768,19,128]{2,1,0:T(8,128)(2,1)}), bf16[768,19,128]{2,1,0:T(8,128)(2,1)}, u32[]{:S(2)}, u32[]{:S(2)}) async-start(bf16[768,19,128]{2,1,0:T(8,128)(2,1)} %copy.19), calls=%async_computation | async-start | bytes 9437184 | tf_op jit(solution)/shard_map/all_to_all | solution.py:118
  36.2 56.8 %collective-permute-start = (f32[3,9,16,1]{3,2,1,0:T(8,128)S(1)}, f32[3,9,16,1]{3,2,1,0:T(8,128)S(1)}, u32[]{:S(2)}, u32[]{:S(2)}) collective-permute-start(f32[3,9,16,1]{3,2,1,0:T(8,128)S(1)} %bitcast.95), channel_id=1, source_target_pairs={{1,0},{2,1},{3,2},{4,3},{5,4},{6,5},{7,6},{8,7},{9,8},{10,9},{11,1... | collective-permute-start | bytes 5192 | tf_op jit(solution)/shard_map/ppermute | solution.py:22
  93.2 3.5 %collective-permute-start.1 = (f32[2,3,9,1,128]{4,3,2,1,0:T(1,128)S(1)}, f32[2,3,9,1,128]{4,3,2,1,0:T(1,128)S(1)}, u32[]{:S(2)}, u32[]{:S(2)}) collective-permute-start(f32[2,3,9,1,128]{4,3,2,1,0:T(1,128)S(1)} %pad_maximum_fusion.11), channel_id=1, source_target_pairs={{16,0},{32,16},{48,32},{64,48},{80,64},{96,80},{112,96},{17,1},{33... | collective-permute-start | bytes 82952 | tf_op jit(solution)/shard_map/ppermute | solution.py:22
  109.4 1.1 copy-start.2
  109.4 1.1 copy-start.3
  111.1 16.2 %collective-permute-start.2 = (f32[2,3,9,16,1]{4,3,2,1,0:T(8,128)S(1)}, f32[2,3,9,16,1]{4,3,2,1,0:T(8,128)S(1)}, u32[]{:S(2)}, u32[]{:S(2)}) collective-permute-start(f32[2,3,9,16,1]{4,3,2,1,0:T(8,128)S(1)} %slice_maximum_fusion.2), channel_id=1, source_target_pairs={{0,1},{1,2},{2,3},{3,4},{4,5},{5,6},{6,7},{7,8},{8,9},{9,10},{10,1... | collective-permute-start | bytes 10376 | tf_op jit(solution)/shard_map/ppermute | solution.py:22
  115.0 15.2 %copy-start.7 = (s32[36]{0:T(128)S(1)}, s32[36]{0:T(128)}, u32[]{:S(2)}) copy-start(s32[36]{0:T(128)} %param.19) | copy-start | bytes 436
  115.1 15.2 %copy-start.8 = (s32[36]{0:T(128)S(1)}, s32[36]{0:T(128)}, u32[]{:S(2)}) copy-start(s32[36]{0:T(128)} %param.18) | copy-start | bytes 436
  127.5 5.4 %copy-start.4 = (f32[9,16,128]{2,1,0:T(8,128)S(1)}, f32[9,16,128]{2,1,0:T(8,128)}, u32[]{:S(2)}) copy-start(f32[9,16,128]{2,1,0:T(8,128)} %param.17) | copy-start | bytes 221188
  127.6 5.0 %collective-permute-start.3 = (f32[3,9,1,128]{3,2,1,0:T(1,128)S(1)}, f32[3,9,1,128]{3,2,1,0:T(1,128)S(1)}, u32[]{:S(2)}, u32[]{:S(2)}) collective-permute-start(f32[3,9,1,128]{3,2,1,0:T(1,128)S(1)} %slice.419), channel_id=1, source_target_pairs={{0,16},{16,32},{32,48},{48,64},{64,80},{80,96},{96,112},{1,17},{17... | collective-permute-start | bytes 41480 | tf_op jit(solution)/shard_map/ppermute | solution.py:22
  133.0 9.1 %collective-permute-start.4 = (f32[3,9,16,1]{3,2,1,0:T(8,128)S(1)}, f32[3,9,16,1]{3,2,1,0:T(8,128)S(1)}, u32[]{:S(2)}, u32[]{:S(2)}) collective-permute-start(f32[3,9,16,1]{3,2,1,0:T(8,128)S(1)} %bitcast.91), channel_id=1, source_target_pairs={{1,0},{2,1},{3,2},{4,3},{5,4},{6,5},{7,6},{8,7},{9,8},{10,9},{11,1... | collective-permute-start | bytes 5192 | tf_op jit(solution)/shard_map/ppermute | solution.py:22
  142.3 3.5 %collective-permute-start.5 = (f32[2,3,9,1,128]{4,3,2,1,0:T(1,128)S(1)}, f32[2,3,9,1,128]{4,3,2,1,0:T(1,128)S(1)}, u32[]{:S(2)}, u32[]{:S(2)}) collective-permute-start(f32[2,3,9,1,128]{4,3,2,1,0:T(1,128)S(1)} %pad_maximum_fusion.10), channel_id=1, source_target_pairs={{16,0},{32,16},{48,32},{64,48},{80,64},{96,80},{112,96},{17,1},{33... | collective-permute-start | bytes 82952 | tf_op jit(solution)/shard_map/ppermute | solution.py:22
  147.1 17.0 %collective-permute-start.6 = (f32[2,3,9,16,1]{4,3,2,1,0:T(8,128)S(1)}, f32[2,3,9,16,1]{4,3,2,1,0:T(8,128)S(1)}, u32[]{:S(2)}, u32[]{:S(2)}) collective-permute-start(f32[2,3,9,16,1]{4,3,2,1,0:T(8,128)S(1)} %slice_maximum_fusion), channel_id=1, source_target_pairs={{0,1},{1,2},{2,3},{3,4},{4,5},{5,6},{6,7},{7,8},{8,9},{9,10},{10,1... | collective-permute-start | bytes 10376 | tf_op jit(solution)/shard_map/ppermute | solution.py:22
  164.3 5.0 %collective-permute-start.7 = (f32[3,9,1,128]{3,2,1,0:T(1,128)S(1)}, f32[3,9,1,128]{3,2,1,0:T(1,128)S(1)}, u32[]{:S(2)}, u32[]{:S(2)}) collective-permute-start(f32[3,9,1,128]{3,2,1,0:T(1,128)S(1)} %slice.453), channel_id=1, source_target_pairs={{0,16},{16,32},{32,48},{48,64},{64,80},{80,96},{96,112},{1,17},{17... | collective-permute-start | bytes 41480 | tf_op jit(solution)/shard_map/ppermute | solution.py:22
  166.3 3.8 %copy-start.5 = (f32[19,8,16,128]{3,2,1,0:T(8,128)}, f32[19,8,16,128]{3,2,1,0:T(8,128)S(1)}, u32[]{:S(2)}) copy-start(f32[19,8,16,128]{3,2,1,0:T(8,128)S(1)} %add_dynamic-update-slice_fusion) | copy-start | bytes 3735556
where the time goes:
time: 171 us; the launch traced here: 170 us
  waiting for transfers between devices  93.6 us (55%)
  starting transfers between devices  31.8 us (19%)
  local copies, waits for them, and re-layouts  29.5 us (17%)
  matrix products  7.59 us (4%)
  other arithmetic  6.45 us (4%)
    ppermute x8, waiting for transfers between devices, passed_along(): lax.ppermute(value, axis, [(source, source + steps) for source in range(i...  93.6 us
    gather x2, local copies, waits for them, and re-layouts, body(): departing_blocks = old_state[send_block[0]]  23.9 us
    ppermute x8, starting transfers between devices, passed_along(): lax.ppermute(value, axis, [(source, source + steps) for source in range(i...  21.2 us
    all_to_all x1, starting transfers between devices, body(): lax.all_to_all(departing_blocks, ('gx', 'gy'), split_axis=0, concat_axis=...  10.6 us
    dot_general x1, matrix products, body(): jnp.einsum('fylt,fyat->lfa', picked_entries, interpolation_weight_tiles,...  7.38 us
    gather x1, local copies, waits for them, and re-layouts, body(): picked_entries = arrived[receive_slot_table]  3.58 us
  transfers between devices with their start and end apart: 9, of which 8 were waited for; matrix products, arithmetic and copies ran while one was open for 2% of the time, Pallas kernels for 0%

commit v1 on v0

v1 whole, which is shorter than its diff:
```python
import jax
import jax.numpy as jnp
from jax import lax
from jax.experimental import pallas as pl
from jax.experimental.pallas import tpu as pltpu
from jax.sharding import PartitionSpec as P

SHEAR = 1.0
BULK = 2.0
YIELD_STRESS = 2.0
HARD_ISO = 0.3
HARD_KIN = 0.5
TIME_STEP = 0.2
PEAK_PRESSURE = 1.5
RADIUS_SQUARED = 36.0

MESH = pl.DeviceIdType.MESH
F32 = jnp.float32
BF16 = jnp.bfloat16

GROUPS = ((0, 7, "x", "y", "z"), (7, 6, "y", "z", "x"), (13, 6, "z", "x", "y"))
DIM = {"z": 0, "y": 2, "x": 3}
SPOTS = 36
NODES = 27


def iota(shape, dim):
    return lax.broadcasted_iota(jnp.int32, shape, dim)


def kernel(
    old, idx, ridx, w, vel, mass, spot_x, spot_y,
    st, vout,
    h0, h1, h2, s0, s1, s2, u0, u1, u2, g0, g1, g2,
    ibuf, psel, qsel, xs, wv, rem,
    vext, vcol, dtm, dtmc, press, pressc, ddx, ddy, dsm, s6, fm, cl, cr,
    rowpack, rowin, colpack, colin, corin,
    row_up, row_dn, row_up_in, row_dn_in, cl_in, cr_in, diag_in,
    cr2, row2, cr2_in, row2_in, diag2_in,
    p1_s, p1_r, ix_s, ix_r, p2_s, p2_r, p3_s, p3_r, loc1, loc2, loc3, wsem,
    hs, hr, e1_s, e1_r, e2_s, e2_r,
):
    hbuf, sbuf, ubuf, gbuf = (h0, h1, h2), (s0, s1, s2), (u0, u1, u2), (g0, g1, g2)
    di = lax.axis_index("gx")
    dj = lax.axis_index("gy")
    here = {"z": di // 2, "c": di % 2, "y": dj // 4, "x": dj % 4}

    def device(**moved):
        at = dict(here)
        for axis, step in moved.items():
            size = 2 if axis == "c" else 4
            at[axis] = (at[axis] + step) % size
        return (at["z"] * 2 + at["c"], at["y"] * 4 + at["x"])

    def plate(a, b):
        return ((di + a + 8) % 8, (dj + b + 16) % 16)

    around = [(a, b) for a in (-1, 0, 1) for b in (-1, 0, 1) if (a, b) != (0, 0)]
    partners = [device(**{axis: d, "c": c}) for axis in "xyz" for d in (1, 2, 3) for c in (0, 1)]
    partners.append(device(c=1))
    partners += [plate(a, b) for a, b in around]
    barrier = pltpu.get_barrier_semaphore()
    for partner in partners:
        pl.semaphore_signal(barrier, inc=1, device_id=partner, device_id_type=MESH)

    def remote(src, dst, ssem, rsem, target):
        return pltpu.make_async_remote_copy(
            src_ref=src, dst_ref=dst, send_sem=ssem, recv_sem=rsem, device_id=target, device_id_type=MESH
        )

    local1 = []
    for q, (first, count, ga, pa, qa) in enumerate(GROUPS):
        mine = here[ga]
        local1.append((
            pltpu.make_async_copy(old.at[pl.ds(first, count)], hbuf[q].at[mine], loc1.at[q, 0]),
            pltpu.make_async_copy(idx.at[q, mine], ibuf.at[q, mine], loc1.at[q, 1]),
        ))
        for copy in local1[-1]:
            copy.start()
    pl.semaphore_wait(barrier, len(partners))

    phase1 = []
    for d in (1, 2, 3):
        for q, (first, count, ga, pa, qa) in enumerate(GROUPS):
            mine = here[ga]
            target = device(**{ga: d})
            tg = (mine + d) % 4
            pair = (
                remote(idx.at[q, tg], ibuf.at[q, mine], ix_s.at[q, d - 1], ix_r.at[q, d - 1], target),
                remote(old.at[pl.ds(first, count)], hbuf[q].at[mine], p1_s.at[q, d - 1], p1_r.at[q, d - 1], target),
            )
            for copy in pair:
                copy.start()
            phase1.append((q, pair))

    weights = [
        pltpu.make_async_copy(w.at[pl.ds(n * 32, 32)], wv.at[pl.ds(n * 32, 32)], wsem.at[n]) for n in range(4)
    ]
    for copy in weights:
        copy.start()

    lane16 = iota((16, 128), 1)
    packed = jnp.zeros((16, 128), F32)
    for n in range(NODES):
        plane = vel[n]
        rowpack[n:n + 1, :] = plane[0:1, :]
        moved = plane if n == 0 else pltpu.roll(plane, n, 1)
        packed = jnp.where(lane16 == n, moved, packed)
        heavy = pltpu.roll(mass[n % 9], n + 32, 1)
        packed = jnp.where(lane16 == n + 32, heavy, packed)
    colpack[...] = packed
    for n in range(9):
        rowpack[32 + n:33 + n, :] = mass[n, 0:1, :]
    halo = (
        remote(rowpack, rowin, hs.at[0], hr.at[0], plate(-1, 0)),
        remote(colpack, colin, hs.at[1], hr.at[1], plate(0, -1)),
        remote(colpack.at[pl.ds(0, 8)], corin, hs.at[2], hr.at[2], plate(-1, -1)),
    )
    for copy in halo:
        copy.start()

    ridx_t = jnp.transpose(ridx[...])
    for q in range(3):
        for k in range(3):
            column = ridx_t[:, q * 3 + k:q * 3 + k + 1]
            for m in range(6):
                hit = column == (iota((128, 128), 1) + m * 128).astype(F32)
                qsel[q, k * 128:(k + 1) * 128, m * 128:(m + 1) * 128] = jnp.where(hit, 1.0, 0.0).astype(BF16)

    row24 = iota((24, 128), 0)
    lane24 = iota((24, 128), 1)
    node_x = (di * 16 + row24).astype(F32)
    node_y = (dj * 128 + lane24).astype(F32)
    next_y = (dj * 128 + 128).astype(F32)

    def spot(n, sums):
        main, side = sums
        sx = spot_x[n].astype(F32)
        sy = spot_y[n].astype(F32)
        far_x = (node_x - sx) ** 2
        main = main + jnp.exp(-(far_x + (node_y - sy) ** 2) / RADIUS_SQUARED)
        side = side + jnp.exp(-(far_x + (next_y - sy) ** 2) / RADIUS_SQUARED)
        return (main, side)

    main, side = lax.fori_loop(0, SPOTS, spot, (jnp.zeros((24, 128), F32), jnp.zeros((24, 128), F32)))
    press[...] = -PEAK_PRESSURE * main
    pressc[...] = jnp.where(lane24 == NODES - 1, -PEAK_PRESSURE * side, 0.0)

    phase2 = []
    for q, (first, count, ga, pa, qa) in enumerate(GROUPS):
        for copy in local1[q]:
            copy.wait()
        for of, pair in phase1:
            if of == q:
                for copy in pair:
                    copy.wait_recv()
        table = jnp.concatenate([ibuf[q].reshape(32, 128), jnp.zeros((96, 128), F32)], axis=0)
        table_t = jnp.transpose(table)
        lanes = iota((128, 128), 1).astype(F32)
        for sg in range(4):
            for rc in range(6):
                hit = table_t[:, sg * 8 + rc:sg * 8 + rc + 1] == lanes
                psel[rc * 128:(rc + 1) * 128, sg * 128:(sg + 1) * 128] = jnp.where(hit, 1.0, 0.0).astype(BF16)
        for half in range(2):
            pick = psel[half * 384:(half + 1) * 384, :]
            for comp in range(count):
                blocks = hbuf[q][:, comp].reshape(512, 128)
                rows = jnp.dot(pick, blocks, preferred_element_type=F32)
                for t in range(16):
                    sbuf[q][half * 2 + t // 8, t % 8, :, comp * 128:(comp + 1) * 128] = rows[
                        t * 24:(t + 1) * 24
                    ].astype(BF16)
        mine = here[pa]
        own = pltpu.make_async_copy(sbuf[q].at[mine], ubuf[q].at[mine], loc2.at[q])
        own.start()
        copies = [
            remote(sbuf[q].at[(mine + d) % 4], ubuf[q].at[mine], p2_s.at[q, d - 1], p2_r.at[q, d - 1], device(**{pa: d}))
            for d in (1, 2, 3)
        ]
        for copy in copies:
            copy.start()
        phase2.append((own, copies))

    for copy in halo:
        copy.wait_recv()
    low_i, high_i = (di > 0).astype(F32), (di < 7).astype(F32)
    low_j, high_j = (dj > 0).astype(F32), (dj < 15).astype(F32)
    first8 = iota((8, 128), 0) == 0
    row_mask = jnp.where(row24 < 16, 1.0, high_i)
    for n in range(NODES):
        vext[n, 0:16, :] = vel[n]
        vext[n, 16:24, :] = jnp.where(first8, rowin[n:n + 1, :] * high_i, 0.0)
    for n in range(9):
        dtm[n, 0:16, :] = TIME_STEP / mass[n]
        dtm[n, 16:24, :] = jnp.where(first8, high_i * TIME_STEP / rowin[32 + n:33 + n, :], 0.0)
    column = jnp.concatenate([colin[...], jnp.where(first8, corin[...] * high_i, 0.0)], axis=0)
    vcol[...] = jnp.where(lane24 < NODES, column * high_j, 0.0)
    heavy = pltpu.roll(jnp.concatenate([colin[...], corin[...]], axis=0), 96, 1)
    used = (lane24 < NODES) & (row24 < 17)
    dtmc[...] = jnp.where(used, high_j * row_mask * TIME_STEP / jnp.where(used, heavy, 1.0), 0.0)

    def differences():
        edge = lane24 == 127
        for n in range(NODES):
            v = vext[n]
            right = jnp.where(edge, vcol[:, n:n + 1], pltpu.roll(v, 127, 1))
            total = v + right
            delta = right - v
            total_up = pltpu.roll(total, 23, 0)
            delta_up = pltpu.roll(delta, 23, 0)
            ddx[n] = (total_up - total)[0:16]
            ddy[n] = (delta_up + delta)[0:16]
            dsm[n] = (total_up + total)[0:16]

    differences()
    for comp in range(6):
        s6[comp, 0] = jnp.zeros((16, 128), F32)
        s6[comp, 9] = jnp.zeros((16, 128), F32)

    phase3 = []
    for q, (first, count, ga, pa, qa) in enumerate(GROUPS):
        own, copies = phase2[q]
        own.wait()
        for copy in copies:
            copy.wait_recv()
        mine = here[qa] * 2 + here["c"]
        own = pltpu.make_async_copy(ubuf[q].at[:, mine], gbuf[q].at[mine], loc3.at[q])
        own.start()
        copies = []
        for d in (2, 1, 3, 0):
            for c in (0, 1):
                if (d, c) != (0, 0):
                    there = ((here[qa] + d) % 4) * 2 + (here["c"] + c) % 2
                    slot = d * 2 + c - 1
                    copies.append(remote(
                        ubuf[q].at[:, there], gbuf[q].at[mine], p3_s.at[q, slot], p3_r.at[q, slot], device(**{qa: d, "c": c})
                    ))
        for copy in copies:
            copy.start()
        phase3.append((own, copies))

    for q, (first, count, ga, pa, qa) in enumerate(GROUPS):
        own, copies = phase3[q]
        own.wait()
        for copy in copies:
            copy.wait_recv()
        for comp in range(count):
            rows = gbuf[q][:, :, :, comp * 128:(comp + 1) * 128].astype(F32).reshape(768, 128).astype(BF16)
            xs[pl.ds(first + comp, 384, stride=24), :] = jnp.dot(qsel[q], rows, preferred_element_type=F32)

    for copy in weights:
        copy.wait()

    def block(g, carry):
        total = jnp.zeros((24, 128), F32)
        for k in range(3):
            start = pl.multiple_of((k * 128 + g) * 24, 8)
            part = xs[pl.ds(start, 24), :].astype(BF16)
            total = total + lax.dot_general(part, wv[g, k], (((1,), (1,)), ((), ())), preferred_element_type=F32)
        rem[pl.ds(pl.multiple_of(g * 24, 8), 24), :] = total
        return carry

    lax.fori_loop(0, 128, block, 0, unroll=4)

    def elements(step):
        def layer(z, carry):
            def state(n):
                if step == 0:
                    return rem[pl.ds(z * 384 + n, 16, stride=24), :]
                return st[n, z]

            gx = [0.25 * (ddx[n * 9 + z] + ddx[n * 9 + z + 1]) for n in range(3)]
            gy = [0.25 * (ddy[n * 9 + z] + ddy[n * 9 + z + 1]) for n in range(3)]
            gz = [0.25 * (dsm[n * 9 + z + 1] - dsm[n * 9 + z]) for n in range(3)]
            strain = [
                TIME_STEP * gx[0],
                TIME_STEP * gy[1],
                TIME_STEP * gz[2],
                TIME_STEP * 0.5 * (gy[0] + gx[1]),
                TIME_STEP * 0.5 * (gz[1] + gy[2]),
                TIME_STEP * 0.5 * (gx[2] + gz[0]),
            ]
            trace = strain[0] + strain[1] + strain[2]
            lame = BULK - 2.0 * SHEAR / 3.0
            trial = []
            for n in range(6):
                value = state(n) + 2.0 * SHEAR * strain[n]
                if n < 3:
                    value = value + lame * trace
                trial.append(value)
            mean = (trial[0] + trial[1] + trial[2]) * (1.0 / 3.0)
            back = [state(6 + n) for n in range(6)]
            xi = [(trial[n] - mean if n < 3 else trial[n]) - back[n] for n in range(6)]
            norm = xi[0] ** 2 + xi[1] ** 2 + xi[2] ** 2 + 2.0 * (xi[3] ** 2 + xi[4] ** 2 + xi[5] ** 2)
            equiv = jnp.sqrt(1.5 * norm)
            epbar = state(18)
            excess = jnp.maximum(equiv - (YIELD_STRESS + HARD_ISO * epbar), 0.0)
            dgamma = excess * (1.0 / (3.0 * SHEAR + HARD_ISO + HARD_KIN))
            factor = dgamma / jnp.maximum(equiv, YIELD_STRESS)
            for n in range(6):
                shift = factor * xi[n]
                stress = trial[n] - 3.0 * SHEAR * shift
                plastic = state(12 + n) + 1.5 * shift
                st[n, z] = stress
                s6[n, z + 1] = stress
                st[6 + n, z] = back[n] + HARD_KIN * shift
                st[12 + n, z] = plastic
            st[18, z] = epbar + dgamma
            return carry

        lax.fori_loop(0, 8, layer, 0)

    along = ((0, 3, 5), (3, 1, 4), (5, 4, 2))
    inner = lane16 > 0
    zeros8 = jnp.zeros((8, 128), F32)

    def forces(last):
        right0 = jnp.zeros((16, 128), F32)
        right1 = jnp.zeros((16, 128), F32)
        left = jnp.zeros((24, 128), F32)
        for i in range(3):
            for k in range(9):
                n = i * 9 + k
                ax = -0.25 * (s6[along[0][i], k + 1] + s6[along[0][i], k])
                ay = -0.25 * (s6[along[1][i], k + 1] + s6[along[1][i], k])
                az = -0.25 * (s6[along[2][i], k] - s6[along[2][i], k + 1])
                near, far = az - ax, az + ax
                near_up, far_up = near + ay, far + ay
                roll0, roll1 = pltpu.roll(near_up, 1, 1), pltpu.roll(far_up, 1, 1)
                e0 = near - ay + jnp.where(inner, roll0, 0.0)
                e1 = far - ay + jnp.where(inner, roll1, 0.0)
                turn0 = roll0 if n == 0 else pltpu.roll(near_up, n + 1, 1)
                turn1 = roll1 if n == 0 else pltpu.roll(far_up, n + 1, 1)
                right0 = jnp.where(lane16 == n, turn0, right0)
                right1 = jnp.where(lane16 == n, turn1, right1)
                whole = jnp.concatenate([e0, zeros8], axis=0) + pltpu.roll(jnp.concatenate([e1, zeros8], axis=0), 1, 0)
                fm[n] = whole
                if last:
                    row2[n:n + 1, :] = whole[16:17]
                else:
                    row_up[n:n + 1, :] = whole[16:17]
                    row_dn[n:n + 1, :] = whole[0:1]
                    left = jnp.where(lane24 == n, whole if n == 0 else pltpu.roll(whole, n, 1), left)
        right = jnp.concatenate([right0, zeros8], axis=0) + pltpu.roll(jnp.concatenate([right1, zeros8], axis=0), 1, 0)
        return left, right

    elements(0)
    left, right = forces(False)
    cl[...] = left
    cr[...] = right
    row_up[32:40, :] = right[16:24]
    row_dn[32:40, :] = right[0:8]
    low, high = pl.ds(0, 8), pl.ds(16, 8)
    round1 = (
        remote(row_up, row_up_in, e1_s.at[0], e1_r.at[0], plate(1, 0)),
        remote(row_dn, row_dn_in, e1_s.at[1], e1_r.at[1], plate(-1, 0)),
        remote(cr, cr_in, e1_s.at[2], e1_r.at[2], plate(0, 1)),
        remote(cl, cl_in, e1_s.at[3], e1_r.at[3], plate(0, -1)),
        remote(cr.at[high], diag_in.at[0], e1_s.at[4], e1_r.at[4], plate(1, 1)),
        remote(cr.at[low], diag_in.at[1], e1_s.at[5], e1_r.at[5], plate(-1, 1)),
        remote(cl.at[high], diag_in.at[2], e1_s.at[6], e1_r.at[6], plate(1, -1)),
        remote(cl.at[low], diag_in.at[3], e1_s.at[7], e1_r.at[7], plate(-1, -1)),
    )
    for copy in round1:
        copy.start()
    for copy in round1:
        copy.wait_recv()

    def ends(at_low, at_high):
        return jnp.concatenate([
            jnp.where(first8, at_low * low_i, 0.0), zeros8, jnp.where(first8, at_high * high_i, 0.0)
        ], axis=0)

    add_left = low_j * (cr_in[...] + ends(diag_in[0], diag_in[1]))
    add_right = high_j * (cl_in[...] + ends(diag_in[2], diag_in[3]))
    col_force = cr[...] + add_right + ends(row_up_in[32:40], row_dn_in[32:40]) + pressc[...]
    vcol[...] = vcol[...] + col_force * dtmc[...]
    for n in range(NODES):
        rows = jnp.concatenate([
            jnp.where(first8, row_up_in[n:n + 1] * low_i, 0.0), zeros8, jnp.where(first8, row_dn_in[n:n + 1] * high_i, 0.0)
        ], axis=0)
        force = fm[n] + rows + jnp.where(lane24 == 0, add_left[:, n:n + 1], 0.0)
        if n == NODES - 1:
            force = force + press[...]
        vext[n] = vext[n] + force * dtm[n % 9]

    differences()
    elements(1)
    left, right = forces(True)
    cr2[...] = right
    round2 = (
        remote(row2, row2_in, e2_s.at[0], e2_r.at[0], plate(1, 0)),
        remote(cr2, cr2_in, e2_s.at[1], e2_r.at[1], plate(0, 1)),
        remote(cr2.at[high], diag2_in, e2_s.at[2], e2_r.at[2], plate(1, 1)),
    )
    for copy in round2:
        copy.start()
    for copy in round2:
        copy.wait_recv()
    corner = jnp.concatenate([jnp.where(first8, diag2_in[...] * low_i, 0.0), zeros8], axis=0)
    add_left = low_j * (cr2_in[0:16] + corner)
    for n in range(NODES):
        rows = jnp.concatenate([jnp.where(first8, row2_in[n:n + 1] * low_i, 0.0), zeros8], axis=0)
        force = fm[n, 0:16] + rows + jnp.where(lane16 == 0, add_left[:, n:n + 1], 0.0)
        if n == NODES - 1:
            force = force + press[0:16]
        vout[n] = vext[n, 0:16] + force * dtm[n % 9, 0:16]

    for q, pair in phase1:
        for copy in pair:
            copy.wait_send()
    for own, copies in phase2 + phase3:
        for copy in copies:
            copy.wait_send()
    for copy in halo + round1 + round2:
        copy.wait_send()


def body(
    old_state,
    send_block,
    receive_slot_table,
    interpolation_weight_tiles,
    velocity,
    node_mass,
    spot_x,
    spot_y,
):
    di, dj = lax.axis_index("gx"), lax.axis_index("gy")
    here = {"z": di // 2, "y": dj // 4, "x": dj % 4}
    wanted = send_block.reshape(4, 2, 4, 4, 6).astype(F32)
    asked = receive_slot_table.T
    source, slot = asked // 6, asked % 6
    place = {"z": source // 32, "c": (source // 16) % 2, "y": (source // 4) % 4, "x": source % 4}
    tables, rows = [], []
    for first, count, ga, pa, qa in GROUPS:
        table = wanted.transpose(DIM[ga], DIM[pa], DIM[qa], 1, 4).reshape(4, 32, 1, 6)
        table = jnp.where(jnp.arange(4)[:, None] == here[ga], table, 255.0).reshape(4, 6, 128)
        tables.append(jnp.pad(table, ((0, 0), (0, 2), (0, 0))))
        rows.append(((place[qa] * 2 + place["c"]) * 4 + place[pa]) * 24 + place[ga] * 6 + slot)
    idx = jnp.stack(tables)
    ridx = jnp.pad(jnp.concatenate(rows).astype(F32), ((0, 119), (0, 0)))

    vmem = pl.BlockSpec(memory_space=pltpu.VMEM)
    smem = pl.BlockSpec(memory_space=pltpu.SMEM)
    anywhere = pl.BlockSpec(memory_space=pl.ANY)
    counts = [group[1] for group in GROUPS]
    scratch = (
        [pltpu.VMEM((4, n, 128, 128), BF16) for n in counts]
        + [pltpu.VMEM((4, 8, 24, n * 128), BF16) for n in counts]
        + [pltpu.VMEM((4, 8, 24, n * 128), BF16) for n in counts]
        + [pltpu.VMEM((8, 4, 24, n * 128), BF16) for n in counts]
        + [
            pltpu.VMEM((3, 4, 8, 128), F32),
            pltpu.VMEM((768, 512), BF16),
            pltpu.VMEM((3, 384, 768), BF16),
            pltpu.VMEM((384 * 24, 128), F32),
            pltpu.VMEM((128, 3, 128, 128), BF16),
            pltpu.VMEM((128 * 24, 128), F32),
            pltpu.VMEM((27, 24, 128), F32),
            pltpu.VMEM((24, 128), F32),
            pltpu.VMEM((9, 24, 128), F32),
            pltpu.VMEM((24, 128), F32),
            pltpu.VMEM((24, 128), F32),
            pltpu.VMEM((24, 128), F32),
            pltpu.VMEM((27, 16, 128), F32),
            pltpu.VMEM((27, 16, 128), F32),
            pltpu.VMEM((27, 16, 128), F32),
            pltpu.VMEM((6, 10, 16, 128), F32),
            pltpu.VMEM((27, 24, 128), F32),
            pltpu.VMEM((24, 128), F32),
            pltpu.VMEM((24, 128), F32),
            pltpu.VMEM((48, 128), F32),
            pltpu.VMEM((48, 128), F32),
            pltpu.VMEM((16, 128), F32),
            pltpu.VMEM((16, 128), F32),
            pltpu.VMEM((8, 128), F32),
            pltpu.VMEM((40, 128), F32),
            pltpu.VMEM((40, 128), F32),
            pltpu.VMEM((40, 128), F32),
            pltpu.VMEM((40, 128), F32),
            pltpu.VMEM((24, 128), F32),
            pltpu.VMEM((24, 128), F32),
            pltpu.VMEM((4, 8, 128), F32),
            pltpu.VMEM((24, 128), F32),
            pltpu.VMEM((32, 128), F32),
            pltpu.VMEM((24, 128), F32),
            pltpu.VMEM((32, 128), F32),
            pltpu.VMEM((8, 128), F32),
        ]
        + [
            pltpu.SemaphoreType.DMA(shape)
            for shape in (
                (3, 3), (3, 3), (3, 3), (3, 3), (3, 3), (3, 3), (3, 7), (3, 7), (3, 2), (3,), (3,), (4,),
                (3,), (3,), (8,), (8,), (3,), (3,),
            )
        ]
    )
    state, moved = pl.pallas_call(
        kernel,
        out_shape=(
            jax.ShapeDtypeStruct((19, 8, 16, 128), F32),
            jax.ShapeDtypeStruct((27, 16, 128), F32),
        ),
        in_specs=[anywhere, vmem, vmem, anywhere, vmem, vmem, smem, smem],
        out_specs=(vmem, vmem),
        scratch_shapes=scratch,
        compiler_params=pltpu.CompilerParams(
            collective_id=0, has_side_effects=True, vmem_limit_bytes=56 * 2**20
        ),
        name="remap_and_steps",
    )(
        old_state.transpose(1, 0, 2),
        idx,
        ridx,
        interpolation_weight_tiles,
        velocity.reshape(27, 16, 128),
        node_mass,
        spot_x,
        spot_y,
    )
    return (state, moved.reshape(3, 9, 16, 128))


def solution(mesh):
    return jax.shard_map(
        body,
        mesh=mesh,
        in_specs=(
            P(("gx", "gy"), None, None),
            P(("gx", "gy"), None),
            P(("gx", "gy"), None),
            P(("gx", "gy"), None, None, None),
            P(None, None, "gx", "gy"),
            P(None, "gx", "gy"),
            P(),
            P(),
        ),
        out_specs=(P(None, None, "gx", "gy"), P(None, None, "gx", "gy")),
        check_vma=False,
    )
```

time: 171 us -> 96.2 us (0.56)
  the two profiles are of different devices: /device:TPU:40 before, /device:TPU:1 now
where the time goes in v1:
time: 96.2 us; the launch traced here: 95.9 us
  Pallas kernels  86.6 us (90%)
  local copies, waits for them, and re-layouts  5.71 us (6%)
  other arithmetic  2.81 us (3%)
    pallas_call x1, Pallas kernels, body(): pl.pallas_call(kernel, out_shape=(jax.ShapeDtypeStruct((19, 8, 16, 128),...  86.6 us
    unnamed x4, local copies, waits for them, and re-layouts  3.17 us

profile of v1, /device:TPU:1, one launch (start us, length us, event | category | flops | bytes accessed | tf_op | source)
XLA Modules:
  0.0 95.9 jit_solution(5823751449506424887)
XLA Ops:
  0.7 0.7 convert_reduce_fusion
  1.4 0.7 add_add_fusion.2
  2.1 0.7 add_add_fusion.1
  2.9 0.1 broadcast_in_dim.82
  2.9 0.1 broadcast_in_dim.83
  3.1 0.1 broadcast_in_dim.76
  3.2 0.1 broadcast_in_dim.77
  3.3 0.1 broadcast_in_dim.69
  3.4 0.1 broadcast_in_dim.70
  3.6 0.6 pad.17.ridx
  4.2 0.2 convert_element_type.16
  4.5 0.3 broadcast_in_dim.81
  4.9 0.3 broadcast_in_dim.74
  5.2 0.3 broadcast_in_dim.87
  5.5 0.6 pad_maximum_fusion.idx
  6.2 86.6 %remap_and_steps.1 = (f32[19,8,16,128]{3,2,1,0:T(8,128)}, f32[27,16,128]{2,1,0:T(8,128)}) custom-call(bf16[19,128,128]{2,1,0:T(8,128)(2,1)} %bitcast.71, f32[3,4,8,128]{3,2,1,0:T(8,128)} %pad_maximum_fusion.idx, f32[128,128]{1,0:T(8,128)} %pad.17.ridx, bf16[128,3,128,128]{3,2,1,0:T(8,128)(2,1)} %w.1, f32[27,16,128]{2,1,0:T(8,128)} %bitcast.76, ...), custom_call_target="tpu_custom_call" | custom-call | tf_op jit(solution)/shard_map/remap_and_steps/pallas_call | solution.py:499
  92.8 0.0 copy-start
  92.8 2.5 %copy.15 = f32[19,8,16,128]{3,2,1,0:T(8,128)} copy(f32[19,8,16,128]{3,2,1,0:T(8,128)} %get-tuple-element.14) | data formatting | bytes 2490368
  95.3 0.0 copy-done
  95.3 0.7 copy.16
  (15 shorter events, 0.3 us)
Async XLA Ops:
  92.8 2.5 %copy-start = (f32[27,16,128]{2,1,0:T(8,128)S(1)}, f32[27,16,128]{2,1,0:T(8,128)}, u32[]{:S(2)}) copy-start(f32[27,16,128]{2,1,0:T(8,128)} %get-tuple-element.5) | copy-start | bytes 663556

commit v2 on v1

--- a/solution.py
+++ b/solution.py
@@ -18,8 +18,9 @@
 F32 = jnp.float32
 BF16 = jnp.bfloat16
 
-GROUPS = ((0, 7, "x", "y", "z"), (7, 6, "y", "z", "x"), (13, 6, "z", "x", "y"))
-DIM = {"z": 0, "y": 2, "x": 3}
+ORDERS = (("x", "y", "z"), ("y", "z", "x"), ("z", "x", "y"))
+CHUNKS = ((0, 4, 0), (4, 3, 1), (7, 3, 2), (10, 3, 0), (13, 3, 1), (16, 3, 2))
+WAVES = ((0, 1, 2), (3, 4, 5))
 SPOTS = 36
 NODES = 27
 
@@ -29,18 +30,20 @@
 
 
 def kernel(
-    old, idx, ridx, w, vel, mass, spot_x, spot_y,
-    st, vout,
-    h0, h1, h2, s0, s1, s2, u0, u1, u2, g0, g1, g2,
-    ibuf, psel, qsel, xs, wv, rem,
-    vext, vcol, dtm, dtmc, press, pressc, ddx, ddy, dsm, s6, fm, cl, cr,
-    rowpack, rowin, colpack, colin, corin,
-    row_up, row_dn, row_up_in, row_dn_in, cl_in, cr_in, diag_in,
-    cr2, row2, cr2_in, row2_in, diag2_in,
-    p1_s, p1_r, ix_s, ix_r, p2_s, p2_r, p3_s, p3_r, loc1, loc2, loc3, wsem,
-    hs, hr, e1_s, e1_r, e2_s, e2_r,
+    old, sends, asks_in, w, vel_in, mass_in, spot_x_in, spot_y_in,
+    st, vout, *scratch,
 ):
-    hbuf, sbuf, ubuf, gbuf = (h0, h1, h2), (s0, s1, s2), (u0, u1, u2), (g0, g1, g2)
+    hbuf, sbuf, ubuf, gbuf = (scratch[n * 6:n * 6 + 6] for n in range(4))
+    (
+        sbuf_in, spread, psel, qsel, xs, wv, rem,
+        vext, vcol, dtm, dtmc, press, pressc, ddx, ddy, dsm, s6, fm, cl, cr,
+        rowpack, rowin, colpack, colin, corin,
+        row_up, row_dn, row_up_in, row_dn_in, cl_in, cr_in, diag_in,
+        cr2, row2, cr2_in, row2_in, diag2_in,
+        asks, vel, mass, spot_x, spot_y,
+        p1_s, p1_r, ix_s, ix_r, p2_s, p2_r, p3_s, p3_r, loc1, locx, loc2, loc3, wsem,
+        hs, hr, e1_s, e1_r, e2_s, e2_r, load,
+    ) = scratch[24:]
     di = lax.axis_index("gx")
     dj = lax.axis_index("gy")
     here = {"z": di // 2, "c": di % 2, "y": dj // 4, "x": dj % 4}
@@ -69,35 +72,54 @@
         )
 
     local1 = []
-    for q, (first, count, ga, pa, qa) in enumerate(GROUPS):
-        mine = here[ga]
-        local1.append((
-            pltpu.make_async_copy(old.at[pl.ds(first, count)], hbuf[q].at[mine], loc1.at[q, 0]),
-            pltpu.make_async_copy(idx.at[q, mine], ibuf.at[q, mine], loc1.at[q, 1]),
-        ))
-        for copy in local1[-1]:
-            copy.start()
+    for q, (first, count, order) in enumerate(CHUNKS):
+        local1.append(
+            pltpu.make_async_copy(old.at[pl.ds(first, count)], hbuf[q].at[here[ORDERS[order][0]]], loc1.at[q])
+        )
+        local1[q].start()
+    localx = []
+    for o, (ga, pa, qa) in enumerate(ORDERS):
+        localx.append(pltpu.make_async_copy(sends, sbuf_in.at[o, here[ga]], locx.at[o]))
+        localx[o].start()
+    pairs = ((vel_in, vel), (mass_in, mass), (asks_in, asks), (spot_x_in, spot_x), (spot_y_in, spot_y))
+    loads = [pltpu.make_async_copy(src, dst, load.at[n]) for n, (src, dst) in enumerate(pairs)]
+    for copy in loads:
+        copy.start()
     pl.semaphore_wait(barrier, len(partners))
 
-    phase1 = []
+    phase1 = {}
+
+    def start_phase1(wave):
+        for q in wave:
+            first, count, order = CHUNKS[q]
+            ga = ORDERS[order][0]
+            phase1[q] = [
+                remote(
+                    old.at[pl.ds(first, count)], hbuf[q].at[here[ga]], p1_s.at[q, d - 1], p1_r.at[q, d - 1], device(**{ga: d})
+                )
+                for d in (1, 2, 3)
+            ]
+        for d in (0, 1, 2):
+            for q in wave:
+                phase1[q][d].start()
+
+    lists = []
     for d in (1, 2, 3):
-        for q, (first, count, ga, pa, qa) in enumerate(GROUPS):
-            mine = here[ga]
-            target = device(**{ga: d})
-            tg = (mine + d) % 4
-            pair = (
-                remote(idx.at[q, tg], ibuf.at[q, mine], ix_s.at[q, d - 1], ix_r.at[q, d - 1], target),
-                remote(old.at[pl.ds(first, count)], hbuf[q].at[mine], p1_s.at[q, d - 1], p1_r.at[q, d - 1], target),
-            )
-            for copy in pair:
-                copy.start()
-            phase1.append((q, pair))
+        for o, (ga, pa, qa) in enumerate(ORDERS):
+            lists.append((o, remote(
+                sends, sbuf_in.at[o, here[ga]], ix_s.at[o, d - 1], ix_r.at[o, d - 1], device(**{ga: d})
+            )))
+            lists[-1][1].start()
+    start_phase1(WAVES[0])
 
     weights = [
         pltpu.make_async_copy(w.at[pl.ds(n * 32, 32)], wv.at[pl.ds(n * 32, 32)], wsem.at[n]) for n in range(4)
     ]
     for copy in weights:
         copy.start()
+
+    for copy in loads:
+        copy.wait()
 
     lane16 = iota((16, 128), 1)
     packed = jnp.zeros((16, 128), F32)
@@ -119,106 +141,65 @@
     for copy in halo:
         copy.start()
 
-    ridx_t = jnp.transpose(ridx[...])
-    for q in range(3):
-        for k in range(3):
-            column = ridx_t[:, q * 3 + k:q * 3 + k + 1]
-            for m in range(6):
-                hit = column == (iota((128, 128), 1) + m * 128).astype(F32)
-                qsel[q, k * 128:(k + 1) * 128, m * 128:(m + 1) * 128] = jnp.where(hit, 1.0, 0.0).astype(BF16)
-
-    row24 = iota((24, 128), 0)
-    lane24 = iota((24, 128), 1)
-    node_x = (di * 16 + row24).astype(F32)
-    node_y = (dj * 128 + lane24).astype(F32)
-    next_y = (dj * 128 + 128).astype(F32)
-
-    def spot(n, sums):
-        main, side = sums
-        sx = spot_x[n].astype(F32)
-        sy = spot_y[n].astype(F32)
-        far_x = (node_x - sx) ** 2
-        main = main + jnp.exp(-(far_x + (node_y - sy) ** 2) / RADIUS_SQUARED)
-        side = side + jnp.exp(-(far_x + (next_y - sy) ** 2) / RADIUS_SQUARED)
-        return (main, side)
-
-    main, side = lax.fori_loop(0, SPOTS, spot, (jnp.zeros((24, 128), F32), jnp.zeros((24, 128), F32)))
-    press[...] = -PEAK_PRESSURE * main
-    pressc[...] = jnp.where(lane24 == NODES - 1, -PEAK_PRESSURE * side, 0.0)
-
-    phase2 = []
-    for q, (first, count, ga, pa, qa) in enumerate(GROUPS):
-        for copy in local1[q]:
-            copy.wait()
-        for of, pair in phase1:
-            if of == q:
-                for copy in pair:
-                    copy.wait_recv()
-        table = jnp.concatenate([ibuf[q].reshape(32, 128), jnp.zeros((96, 128), F32)], axis=0)
-        table_t = jnp.transpose(table)
-        lanes = iota((128, 128), 1).astype(F32)
+    t192, c768 = iota((192, 128), 0), iota((192, 128), 1)
+    aim, part = t192 // 6, t192 % 6
+    on_p, on_q, on_c = aim // 8, (aim // 2) % 4, aim % 2
+    for o, (ga, pa, qa) in enumerate(ORDERS):
+        at = {ga: here[ga], pa: on_p, qa: on_q}
+        stands = (((at["z"] * 2 + on_c) * 4 + at["y"]) * 4 + at["x"]) * 6 + part
+        for m in range(6):
+            spread[o, :, m * 128:(m + 1) * 128] = jnp.where(stands == c768 + m * 128, 1.0, 0.0).astype(BF16)
+    r768 = iota((768, 256), 0)
+    widen = jnp.where((r768 // 24) * 6 + r768 % 6 == iota((768, 256), 1), 1.0, 0.0).astype(BF16)
+    source_of = (iota((768, 128), 0) // 6) % 4
+    lanes768 = iota((768, 128), 1).astype(F32)
+
+    phase2 = {}
+
+    def selection(o):
+        localx[o].wait()
+        for of, copy in lists:
+            if of == o:
+                copy.wait_recv()
+        table = jnp.concatenate(
+            [sbuf_in[o, n].astype(F32) for n in range(4)] + [jnp.zeros((4, 768), F32)], axis=0
+        ).astype(BF16)
+        short = lax.dot_general(spread[o], table, (((1,), (1,)), ((), ())), preferred_element_type=F32)
+        short = jnp.concatenate([short, jnp.zeros((64, 8), F32)], axis=0).astype(BF16)
+        codes = jnp.dot(widen, short, preferred_element_type=F32)
         for sg in range(4):
-            for rc in range(6):
-                hit = table_t[:, sg * 8 + rc:sg * 8 + rc + 1] == lanes
-                psel[rc * 128:(rc + 1) * 128, sg * 128:(sg + 1) * 128] = jnp.where(hit, 1.0, 0.0).astype(BF16)
+            hit = (codes[:, sg:sg + 1] == lanes768) & (source_of == sg)
+            psel[o, :, sg * 128:(sg + 1) * 128] = jnp.where(hit, 1.0, 0.0).astype(BF16)
+
+    def arrived(q):
+        local1[q].wait()
+        for copy in phase1[q]:
+            copy.wait_recv()
+
+    def start_phase2(q):
+        first, count, o = CHUNKS[q]
+        ga, pa, qa = ORDERS[o]
+        blocks = jnp.concatenate([hbuf[q][:, n].reshape(512, 128) for n in range(count)], axis=1)
         for half in range(2):
-            pick = psel[half * 384:(half + 1) * 384, :]
-            for comp in range(count):
-                blocks = hbuf[q][:, comp].reshape(512, 128)
-                rows = jnp.dot(pick, blocks, preferred_element_type=F32)
-                for t in range(16):
-                    sbuf[q][half * 2 + t // 8, t % 8, :, comp * 128:(comp + 1) * 128] = rows[
-                        t * 24:(t + 1) * 24
-                    ].astype(BF16)
+            rows = jnp.dot(psel[o, half * 384:(half + 1) * 384, :], blocks, preferred_element_type=F32)
+            for t in range(16):
+                sbuf[q][half * 2 + t // 8, t % 8] = rows[t * 24:(t + 1) * 24].astype(BF16)
         mine = here[pa]
         own = pltpu.make_async_copy(sbuf[q].at[mine], ubuf[q].at[mine], loc2.at[q])
         own.start()
         copies = [
             remote(sbuf[q].at[(mine + d) % 4], ubuf[q].at[mine], p2_s.at[q, d - 1], p2_r.at[q, d - 1], device(**{pa: d}))
-            for d in (1, 2, 3)
+            for d in (2, 1, 3)
         ]
         for copy in copies:
             copy.start()
-        phase2.append((own, copies))
-
-    for copy in halo:
-        copy.wait_recv()
-    low_i, high_i = (di > 0).astype(F32), (di < 7).astype(F32)
-    low_j, high_j = (dj > 0).astype(F32), (dj < 15).astype(F32)
-    first8 = iota((8, 128), 0) == 0
-    row_mask = jnp.where(row24 < 16, 1.0, high_i)
-    for n in range(NODES):
-        vext[n, 0:16, :] = vel[n]
-        vext[n, 16:24, :] = jnp.where(first8, rowin[n:n + 1, :] * high_i, 0.0)
-    for n in range(9):
-        dtm[n, 0:16, :] = TIME_STEP / mass[n]
-        dtm[n, 16:24, :] = jnp.where(first8, high_i * TIME_STEP / rowin[32 + n:33 + n, :], 0.0)
-    column = jnp.concatenate([colin[...], jnp.where(first8, corin[...] * high_i, 0.0)], axis=0)
-    vcol[...] = jnp.where(lane24 < NODES, column * high_j, 0.0)
-    heavy = pltpu.roll(jnp.concatenate([colin[...], corin[...]], axis=0), 96, 1)
-    used = (lane24 < NODES) & (row24 < 17)
-    dtmc[...] = jnp.where(used, high_j * row_mask * TIME_STEP / jnp.where(used, heavy, 1.0), 0.0)
-
-    def differences():
-        edge = lane24 == 127
-        for n in range(NODES):
-            v = vext[n]
-            right = jnp.where(edge, vcol[:, n:n + 1], pltpu.roll(v, 127, 1))
-            total = v + right
-            delta = right - v
-            total_up = pltpu.roll(total, 23, 0)
-            delta_up = pltpu.roll(delta, 23, 0)
-            ddx[n] = (total_up - total)[0:16]
-            ddy[n] = (delta_up + delta)[0:16]
-            dsm[n] = (total_up + total)[0:16]
-
-    differences()
-    for comp in range(6):
-        s6[comp, 0] = jnp.zeros((16, 128), F32)
-        s6[comp, 9] = jnp.zeros((16, 128), F32)
-
-    phase3 = []
-    for q, (first, count, ga, pa, qa) in enumerate(GROUPS):
+        phase2[q] = (own, copies)
+
+    phase3 = {}
+
+    def start_phase3(q):
+        first, count, o = CHUNKS[q]
+        ga, pa, qa = ORDERS[o]
         own, copies = phase2[q]
         own.wait()
         for copy in copies:
@@ -237,30 +218,129 @@
                     ))
         for copy in copies:
             copy.start()
-        phase3.append((own, copies))
-
-    for q, (first, count, ga, pa, qa) in enumerate(GROUPS):
+        phase3[q] = (own, copies)
+
+    def turn(first, last):
+        def tile(g, carry):
+            for k in range(3):
+                wv[g, k] = wv[g, k].T
+            return carry
+
+        lax.fori_loop(first, last, tile, 0, unroll=4)
+
+    def arrive(q):
+        first, count, o = CHUNKS[q]
         own, copies = phase3[q]
         own.wait()
         for copy in copies:
             copy.wait_recv()
-        for comp in range(count):
-            rows = gbuf[q][:, :, :, comp * 128:(comp + 1) * 128].astype(F32).reshape(768, 128).astype(BF16)
-            xs[pl.ds(first + comp, 384, stride=24), :] = jnp.dot(qsel[q], rows, preferred_element_type=F32)
-
+        rows = gbuf[q][...].astype(F32).reshape(768, count * 128).astype(BF16)
+        picked = jnp.dot(qsel[o], rows, preferred_element_type=F32)
+        for n in range(count):
+            xs[pl.ds(first + n, 384, stride=24), :] = picked[:, n * 128:(n + 1) * 128]
+
+    for o in range(3):
+        selection(o)
+    for q in WAVES[0]:
+        arrived(q)
+    start_phase1(WAVES[1])
+    for q in WAVES[0]:
+        start_phase2(q)
+
+    asked = asks[...]
+    origin = (asked * 10923) >> 16
+    slot = asked - origin * 6
+    place = {"z": origin >> 5, "c": (origin >> 4) & 1, "y": (origin >> 2) & 3, "x": origin & 3}
+    wanted = [
+        (((place[qa] * 2 + place["c"]) * 4 + place[pa]) * 24 + place[ga] * 6 + slot).astype(F32) for ga, pa, qa in ORDERS
+    ]
+    ridx_t = jnp.transpose(jnp.concatenate(wanted + [jnp.zeros((119, 128), F32)], axis=0))
+    for q in range(3):
+        for k in range(3):
+            column = ridx_t[:, q * 3 + k:q * 3 + k + 1]
+            for m in range(6):
+                hit = column == (iota((128, 128), 1) + m * 128).astype(F32)
+                qsel[q, k * 128:(k + 1) * 128, m * 128:(m + 1) * 128] = jnp.where(hit, 1.0, 0.0).astype(BF16)
+
+    row24 = iota((24, 128), 0)
+    lane24 = iota((24, 128), 1)
+    node_x = (di * 16 + row24).astype(F32)
+    node_y = (dj * 128 + lane24).astype(F32)
+    next_y = (dj * 128 + 128).astype(F32)
+
+    def spot(n, sums):
+        main, side = sums
+        sx = spot_x[n].astype(F32)
+        sy = spot_y[n].astype(F32)
+        far_x = (node_x - sx) ** 2
+        main = main + jnp.exp(-(far_x + (node_y - sy) ** 2) / RADIUS_SQUARED)
+        side = side + jnp.exp(-(far_x + (next_y - sy) ** 2) / RADIUS_SQUARED)
+        return (main, side)
+
+    main, side = lax.fori_loop(0, SPOTS, spot, (jnp.zeros((24, 128), F32), jnp.zeros((24, 128), F32)))
+    press[...] = -PEAK_PRESSURE * main
+    pressc[...] = jnp.where(lane24 == NODES - 1, -PEAK_PRESSURE * side, 0.0)
+
+    for q in WAVES[1]:
+        arrived(q)
+        start_phase2(q)
     for copy in weights:
         copy.wait()
+    for q in WAVES[0]:
+        start_phase3(q)
+    turn(0, 64)
+    for q in WAVES[1]:
+        start_phase3(q)
+
+    for copy in halo:
+        copy.wait_recv()
+    low_i, high_i = (di > 0).astype(F32), (di < 7).astype(F32)
+    low_j, high_j = (dj > 0).astype(F32), (dj < 15).astype(F32)
+    first8 = iota((8, 128), 0) == 0
+    row_mask = jnp.where(row24 < 16, 1.0, high_i)
+    for n in range(NODES):
+        vext[n, 0:16, :] = vel[n]
+        vext[n, 16:24, :] = jnp.where(first8, rowin[n:n + 1, :] * high_i, 0.0)
+    for n in range(9):
+        dtm[n, 0:16, :] = TIME_STEP / mass[n]
+        dtm[n, 16:24, :] = jnp.where(first8, high_i * TIME_STEP / rowin[32 + n:33 + n, :], 0.0)
+    column = jnp.concatenate([colin[...], jnp.where(first8, corin[...] * high_i, 0.0)], axis=0)
+    vcol[...] = jnp.where(lane24 < NODES, column * high_j, 0.0)
+    heavy = pltpu.roll(jnp.concatenate([colin[...], corin[...]], axis=0), 96, 1)
+    used = (lane24 < NODES) & (row24 < 17)
+    dtmc[...] = jnp.where(used, high_j * row_mask * TIME_STEP / jnp.where(used, heavy, 1.0), 0.0)
+
+    def differences():
+        edge = lane24 == 127
+        for n in range(NODES):
+            v = vext[n]
+            right = jnp.where(edge, vcol[:, n:n + 1], pltpu.roll(v, 127, 1))
+            total = v + right
+            delta = right - v
+            total_up = pltpu.roll(total, 23, 0)
+            delta_up = pltpu.roll(delta, 23, 0)
+            ddx[n] = (total_up - total)[0:16]
+            ddy[n] = (delta_up + delta)[0:16]
+            dsm[n] = (total_up + total)[0:16]
+
+    differences()
+    for comp in range(6):
+        s6[comp, 0] = jnp.zeros((16, 128), F32)
+        s6[comp, 9] = jnp.zeros((16, 128), F32)
+
+    turn(64, 128)
+    for wave in WAVES:
+        for q in wave:
+            arrive(q)
 
     def block(g, carry):
-        total = jnp.zeros((24, 128), F32)
-        for k in range(3):
-            start = pl.multiple_of((k * 128 + g) * 24, 8)
-            part = xs[pl.ds(start, 24), :].astype(BF16)
-            total = total + lax.dot_general(part, wv[g, k], (((1,), (1,)), ((), ())), preferred_element_type=F32)
-        rem[pl.ds(pl.multiple_of(g * 24, 8), 24), :] = total
+        parts = [xs[pl.ds(pl.multiple_of((k * 128 + g) * 24, 8), 24), :] for k in range(3)]
+        rem[pl.ds(pl.multiple_of(g * 24, 8), 24), :] = jnp.dot(
+            jnp.concatenate(parts, axis=1).astype(BF16), wv[g].reshape(384, 128), preferred_element_type=F32
+        )
         return carry
 
-    lax.fori_loop(0, 128, block, 0, unroll=4)
+    lax.fori_loop(0, 128, block, 0, unroll=8)
 
     def elements(step):
         def layer(z, carry):
@@ -406,11 +486,10 @@
             force = force + press[0:16]
         vout[n] = vext[n, 0:16] + force * dtm[n % 9, 0:16]
 
-    for q, pair in phase1:
-        for copy in pair:
-            copy.wait_send()
-    for own, copies in phase2 + phase3:
-        for copy in copies:
+    for o, copy in lists:
+        copy.wait_send()
+    for q in range(6):
+        for copy in phase1[q] + phase2[q][1] + phase3[q][1]:
             copy.wait_send()
     for copy in halo + round1 + round2:
         copy.wait_send()
@@ -426,33 +505,18 @@
     spot_x,
     spot_y,
 ):
-    di, dj = lax.axis_index("gx"), lax.axis_index("gy")
-    here = {"z": di // 2, "y": dj // 4, "x": dj % 4}
-    wanted = send_block.reshape(4, 2, 4, 4, 6).astype(F32)
-    asked = receive_slot_table.T
-    source, slot = asked // 6, asked % 6
-    place = {"z": source // 32, "c": (source // 16) % 2, "y": (source // 4) % 4, "x": source % 4}
-    tables, rows = [], []
-    for first, count, ga, pa, qa in GROUPS:
-        table = wanted.transpose(DIM[ga], DIM[pa], DIM[qa], 1, 4).reshape(4, 32, 1, 6)
-        table = jnp.where(jnp.arange(4)[:, None] == here[ga], table, 255.0).reshape(4, 6, 128)
-        tables.append(jnp.pad(table, ((0, 0), (0, 2), (0, 0))))
-        rows.append(((place[qa] * 2 + place["c"]) * 4 + place[pa]) * 24 + place[ga] * 6 + slot)
-    idx = jnp.stack(tables)
-    ridx = jnp.pad(jnp.concatenate(rows).astype(F32), ((0, 119), (0, 0)))
-
     vmem = pl.BlockSpec(memory_space=pltpu.VMEM)
-    smem = pl.BlockSpec(memory_space=pltpu.SMEM)
-    anywhere = pl.BlockSpec(memory_space=pl.ANY)
-    counts = [group[1] for group in GROUPS]
+    hbm = pl.BlockSpec(memory_space=pltpu.HBM)
+    counts = [chunk[1] for chunk in CHUNKS]
     scratch = (
         [pltpu.VMEM((4, n, 128, 128), BF16) for n in counts]
         + [pltpu.VMEM((4, 8, 24, n * 128), BF16) for n in counts]
         + [pltpu.VMEM((4, 8, 24, n * 128), BF16) for n in counts]
         + [pltpu.VMEM((8, 4, 24, n * 128), BF16) for n in counts]
         + [
-            pltpu.VMEM((3, 4, 8, 128), F32),
-            pltpu.VMEM((768, 512), BF16),
+            pltpu.VMEM((3, 4, 1, 768), jnp.int32),
+            pltpu.VMEM((3, 192, 768), BF16),
+            pltpu.VMEM((3, 768, 512), BF16),
             pltpu.VMEM((3, 384, 768), BF16),
             pltpu.VMEM((384 * 24, 128), F32),
             pltpu.VMEM((128, 3, 128, 128), BF16),
@@ -487,12 +551,17 @@
             pltpu.VMEM((24, 128), F32),
             pltpu.VMEM((32, 128), F32),
             pltpu.VMEM((8, 128), F32),
+            pltpu.VMEM((3, 128), jnp.int32),
+            pltpu.VMEM((27, 16, 128), F32),
+            pltpu.VMEM((9, 16, 128), F32),
+            pltpu.SMEM((36,), jnp.int32),
+            pltpu.SMEM((36,), jnp.int32),
         ]
         + [
             pltpu.SemaphoreType.DMA(shape)
             for shape in (
-                (3, 3), (3, 3), (3, 3), (3, 3), (3, 3), (3, 3), (3, 7), (3, 7), (3, 2), (3,), (3,), (4,),
-                (3,), (3,), (8,), (8,), (3,), (3,),
+                (6, 3), (6, 3), (3, 3), (3, 3), (6, 3), (6, 3), (6, 7), (6, 7), (6,), (3,), (6,), (6,), (4,),
+                (3,), (3,), (8,), (8,), (3,), (3,), (5,),
             )
         ]
     )
@@ -502,23 +571,26 @@
             jax.ShapeDtypeStruct((19, 8, 16, 128), F32),
             jax.ShapeDtypeStruct((27, 16, 128), F32),
         ),
-        in_specs=[anywhere, vmem, vmem, anywhere, vmem, vmem, smem, smem],
+        in_specs=[hbm] * 8,
         out_specs=(vmem, vmem),
         scratch_shapes=scratch,
         compiler_params=pltpu.CompilerParams(
-            collective_id=0, has_side_effects=True, vmem_limit_bytes=56 * 2**20
+            collective_id=0, has_side_effects=True, vmem_limit_bytes=48 * 2**20
         ),
         name="remap_and_steps",
-    )(
-        old_state.transpose(1, 0, 2),
-        idx,
-        ridx,
-        interpolation_weight_tiles,
-        velocity.reshape(27, 16, 128),
-        node_mass,
-        spot_x,
-        spot_y,
-    )
+    )(*(
+        pltpu.with_memory_space_constraint(array, pltpu.HBM)
+        for array in (
+            old_state.transpose(1, 0, 2),
+            send_block,
+            receive_slot_table.T,
+            interpolation_weight_tiles,
+            velocity.reshape(27, 16, 128),
+            node_mass,
+            spot_x,
+            spot_y,
+        )
+    ))
     return (state, moved.reshape(3, 9, 16, 128))
 
 

time: 96.2 us -> 73.8 us (0.77)
  Pallas kernels: 86.6 us -> 71.3 us
  local copies, waits for them, and re-layouts: 5.71 us -> 1.72 us
  other arithmetic: 2.81 us -> 0 us
    pallas_call x1, Pallas kernels: 86.6 us -> 71.3 us  [body(): pl.pallas_call(kernel, out_shape=(jax.ShapeDtypeStruct((19, 8, 16, 128),...]
    broadcast_in_dim x12 -> x0, local copies, waits for them, and re-layouts: 1.63 us -> none  [body(): jnp.where(jnp.arange(4)[:, None] == here[ga], table, 255.0)]
    unnamed x4 -> x2, local copies, waits for them, and re-layouts: 3.17 us -> 1.72 us
    add x2 -> x0, other arithmetic: 1.44 us -> none  [body(): ((place[qa] * 2 + place['c']) * 4 + place[pa]) * 24 + place[ga] * 6 + slot]
where the time goes in v2:
time: 73.8 us; the launch traced here: 73.7 us
  Pallas kernels  71.3 us (97%)
  local copies, waits for them, and re-layouts  1.72 us (2%)
    pallas_call x1, Pallas kernels, body(): pl.pallas_call(kernel, out_shape=(jax.ShapeDtypeStruct((19, 8, 16, 128),...  71.3 us
    unnamed x2, local copies, waits for them, and re-layouts  1.72 us

profile of v2, /device:TPU:1, one launch (start us, length us, event | category | flops | bytes accessed | tf_op | source)
XLA Modules:
  0.0 73.7 jit_solution(12369527579092956459)
XLA Ops:
  0.6 71.3 %remap_and_steps.1 = (f32[19,8,16,128]{3,2,1,0:T(8,128)S(1)}, f32[27,16,128]{2,1,0:T(8,128)S(1)}) custom-call(bf16[19,128,128]{2,1,0:T(8,128)(2,1)} %bitcast.5, s32[1,768]{1,0:T(1,128)} %sends.1, s32[3,128]{1,0:T(4,128)} %bitcast.7, bf16[128,3,128,128]{3,2,1,0:T(8,128)(2,1)} %w.1, f32[27,16,128]{2,1,0:T(8,128)} %bitcast.6, f32[9,16,128]{2,1,0:T(8,128)} %mass_in.1, ...), custom_call_target="tpu_custom_call" | custom-call | tf_op jit(solution)/shard_map/remap_and_steps/pallas_call | solution.py:568
  71.9 1.0 %copy.12 = f32[19,8,16,128]{3,2,1,0:T(8,128)} copy(f32[19,8,16,128]{3,2,1,0:T(8,128)S(1)} %get-tuple-element.8) | data formatting | bytes 2490368
  73.0 0.7 copy.13

commit v3 on v2

--- a/solution.py
+++ b/solution.py
@@ -31,7 +31,7 @@
 
 def kernel(
     old, sends, asks_in, w, vel_in, mass_in, spot_x_in, spot_y_in,
-    st, vout, *scratch,
+    state_out, v_out, *scratch,
 ):
     hbuf, sbuf, ubuf, gbuf = (scratch[n * 6:n * 6 + 6] for n in range(4))
     (
@@ -40,9 +40,9 @@
         rowpack, rowin, colpack, colin, corin,
         row_up, row_dn, row_up_in, row_dn_in, cl_in, cr_in, diag_in,
         cr2, row2, cr2_in, row2_in, diag2_in,
-        asks, vel, mass, spot_x, spot_y,
+        asks, vel, mass, spot_x, spot_y, st, vout,
         p1_s, p1_r, ix_s, ix_r, p2_s, p2_r, p3_s, p3_r, loc1, locx, loc2, loc3, wsem,
-        hs, hr, e1_s, e1_r, e2_s, e2_r, load,
+        hs, hr, e1_s, e1_r, e2_s, e2_r, load, out_sem,
     ) = scratch[24:]
     di = lax.axis_index("gx")
     dj = lax.axis_index("gy")
@@ -61,7 +61,7 @@
     around = [(a, b) for a in (-1, 0, 1) for b in (-1, 0, 1) if (a, b) != (0, 0)]
     partners = [device(**{axis: d, "c": c}) for axis in "xyz" for d in (1, 2, 3) for c in (0, 1)]
     partners.append(device(c=1))
-    partners += [plate(a, b) for a, b in around]
+    partners += [plate(a, b) for a, b in around if b != 0]
     barrier = pltpu.get_barrier_semaphore()
     for partner in partners:
         pl.semaphore_signal(barrier, inc=1, device_id=partner, device_id_type=MESH)
@@ -87,7 +87,7 @@
         copy.start()
     pl.semaphore_wait(barrier, len(partners))
 
-    phase1 = {}
+    phase1, onward = {}, {}
 
     def start_phase1(wave):
         for q in wave:
@@ -95,13 +95,25 @@
             ga = ORDERS[order][0]
             phase1[q] = [
                 remote(
-                    old.at[pl.ds(first, count)], hbuf[q].at[here[ga]], p1_s.at[q, d - 1], p1_r.at[q, d - 1], device(**{ga: d})
+                    old.at[pl.ds(first, count)], hbuf[q].at[here[ga]], p1_s.at[q, n], p1_r.at[q, n], device(**{ga: d})
                 )
-                for d in (1, 2, 3)
+                for n, d in enumerate((1, 3))
             ]
-        for d in (0, 1, 2):
+        for n in (0, 1):
             for q in wave:
-                phase1[q][d].start()
+                phase1[q][n].start()
+
+    def start_onward(wave):
+        for q in wave:
+            first, count, order = CHUNKS[q]
+            ga = ORDERS[order][0]
+            half = count // 2 if q % 2 == 0 else count - count // 2
+            onward[q] = []
+            for n, (d, back, part) in enumerate(((1, 3, pl.ds(0, half)), (3, 1, pl.ds(half, count - half)))):
+                phase1[q][n].wait_recv()
+                held = hbuf[q].at[(here[ga] + back) % 4, part]
+                onward[q].append(remote(held, held, p1_s.at[q, 2 + n], p1_r.at[q, 2 + n], device(**{ga: d})))
+                onward[q][n].start()
 
     lists = []
     for d in (1, 2, 3):
@@ -111,6 +123,7 @@
             )))
             lists[-1][1].start()
     start_phase1(WAVES[0])
+    start_phase1(WAVES[1])
 
     weights = [
         pltpu.make_async_copy(w.at[pl.ds(n * 32, 32)], wv.at[pl.ds(n * 32, 32)], wsem.at[n]) for n in range(4)
@@ -173,7 +186,7 @@
 
     def arrived(q):
         local1[q].wait()
-        for copy in phase1[q]:
+        for copy in onward[q]:
             copy.wait_recv()
 
     def start_phase2(q):
@@ -239,12 +252,13 @@
         for n in range(count):
             xs[pl.ds(first + n, 384, stride=24), :] = picked[:, n * 128:(n + 1) * 128]
 
-    for o in range(3):
-        selection(o)
+    selection(0)
+    start_onward(WAVES[0])
+    selection(1)
+    selection(2)
+    start_onward(WAVES[1])
     for q in WAVES[0]:
         arrived(q)
-    start_phase1(WAVES[1])
-    for q in WAVES[0]:
         start_phase2(q)
 
     asked = asks[...]
@@ -340,7 +354,7 @@
         )
         return carry
 
-    lax.fori_loop(0, 128, block, 0, unroll=8)
+    lax.fori_loop(0, 128, block, 0, unroll=16)
 
     def elements(step):
         def layer(z, carry):
@@ -432,14 +446,14 @@
     row_dn[32:40, :] = right[0:8]
     low, high = pl.ds(0, 8), pl.ds(16, 8)
     round1 = (
-        remote(row_up, row_up_in, e1_s.at[0], e1_r.at[0], plate(1, 0)),
-        remote(row_dn, row_dn_in, e1_s.at[1], e1_r.at[1], plate(-1, 0)),
-        remote(cr, cr_in, e1_s.at[2], e1_r.at[2], plate(0, 1)),
-        remote(cl, cl_in, e1_s.at[3], e1_r.at[3], plate(0, -1)),
         remote(cr.at[high], diag_in.at[0], e1_s.at[4], e1_r.at[4], plate(1, 1)),
         remote(cr.at[low], diag_in.at[1], e1_s.at[5], e1_r.at[5], plate(-1, 1)),
         remote(cl.at[high], diag_in.at[2], e1_s.at[6], e1_r.at[6], plate(1, -1)),
         remote(cl.at[low], diag_in.at[3], e1_s.at[7], e1_r.at[7], plate(-1, -1)),
+        remote(cr, cr_in, e1_s.at[2], e1_r.at[2], plate(0, 1)),
+        remote(cl, cl_in, e1_s.at[3], e1_r.at[3], plate(0, -1)),
+        remote(row_up, row_up_in, e1_s.at[0], e1_r.at[0], plate(1, 0)),
+        remote(row_dn, row_dn_in, e1_s.at[1], e1_r.at[1], plate(-1, 0)),
     )
     for copy in round1:
         copy.start()
@@ -469,12 +483,14 @@
     left, right = forces(True)
     cr2[...] = right
     round2 = (
+        remote(cr2.at[high], diag2_in, e2_s.at[2], e2_r.at[2], plate(1, 1)),
+        remote(cr2, cr2_in, e2_s.at[1], e2_r.at[1], plate(0, 1)),
         remote(row2, row2_in, e2_s.at[0], e2_r.at[0], plate(1, 0)),
-        remote(cr2, cr2_in, e2_s.at[1], e2_r.at[1], plate(0, 1)),
-        remote(cr2.at[high], diag2_in, e2_s.at[2], e2_r.at[2], plate(1, 1)),
     )
     for copy in round2:
         copy.start()
+    state_copy = pltpu.make_async_copy(st, state_out, out_sem.at[0])
+    state_copy.start()
     for copy in round2:
         copy.wait_recv()
     corner = jnp.concatenate([jnp.where(first8, diag2_in[...] * low_i, 0.0), zeros8], axis=0)
@@ -486,13 +502,17 @@
             force = force + press[0:16]
         vout[n] = vext[n, 0:16] + force * dtm[n % 9, 0:16]
 
+    v_copy = pltpu.make_async_copy(vout, v_out, out_sem.at[1])
+    v_copy.start()
     for o, copy in lists:
         copy.wait_send()
     for q in range(6):
-        for copy in phase1[q] + phase2[q][1] + phase3[q][1]:
+        for copy in phase1[q] + onward[q] + phase2[q][1] + phase3[q][1]:
             copy.wait_send()
     for copy in halo + round1 + round2:
         copy.wait_send()
+    state_copy.wait()
+    v_copy.wait()
 
 
 def body(
@@ -505,7 +525,7 @@
     spot_x,
     spot_y,
 ):
-    vmem = pl.BlockSpec(memory_space=pltpu.VMEM)
+    anywhere = pl.BlockSpec(memory_space=pl.ANY)
     hbm = pl.BlockSpec(memory_space=pltpu.HBM)
     counts = [chunk[1] for chunk in CHUNKS]
     scratch = (
@@ -556,12 +576,14 @@
             pltpu.VMEM((9, 16, 128), F32),
             pltpu.SMEM((36,), jnp.int32),
             pltpu.SMEM((36,), jnp.int32),
+            pltpu.VMEM((19, 8, 16, 128), F32),
+            pltpu.VMEM((27, 16, 128), F32),
         ]
         + [
             pltpu.SemaphoreType.DMA(shape)
             for shape in (
-                (6, 3), (6, 3), (3, 3), (3, 3), (6, 3), (6, 3), (6, 7), (6, 7), (6,), (3,), (6,), (6,), (4,),
-                (3,), (3,), (8,), (8,), (3,), (3,), (5,),
+                (6, 4), (6, 4), (3, 3), (3, 3), (6, 3), (6, 3), (6, 7), (6, 7), (6,), (3,), (6,), (6,), (4,),
+                (3,), (3,), (8,), (8,), (3,), (3,), (5,), (2,),
             )
         ]
     )
@@ -572,7 +594,7 @@
             jax.ShapeDtypeStruct((27, 16, 128), F32),
         ),
         in_specs=[hbm] * 8,
-        out_specs=(vmem, vmem),
+        out_specs=(anywhere, anywhere),
         scratch_shapes=scratch,
         compiler_params=pltpu.CompilerParams(
             collective_id=0, has_side_effects=True, vmem_limit_bytes=48 * 2**20

time: 73.8 us -> 70.8 us (0.959)
  Pallas kernels: 71.3 us -> 68.3 us
    pallas_call x1, Pallas kernels: 71.3 us -> 68.3 us  [body(): pl.pallas_call(kernel, out_shape=(jax.ShapeDtypeStruct((19, 8, 16, 128),...]
where the time goes in v3:
time: 70.8 us; the launch traced here: 70.6 us
  Pallas kernels  68.3 us (96%)
  local copies, waits for them, and re-layouts  1.72 us (2%)
    pallas_call x1, Pallas kernels, body(): pl.pallas_call(kernel, out_shape=(jax.ShapeDtypeStruct((19, 8, 16, 128),...  68.3 us
    unnamed x2, local copies, waits for them, and re-layouts  1.72 us

profile of v3, /device:TPU:1, one launch (start us, length us, event | category | flops | bytes accessed | tf_op | source)
XLA Modules:
  0.0 70.6 jit_solution(15707833390518584451)
XLA Ops:
  0.6 68.3 %remap_and_steps.1 = (f32[19,8,16,128]{3,2,1,0:T(8,128)S(1)}, f32[27,16,128]{2,1,0:T(8,128)S(1)}) custom-call(bf16[19,128,128]{2,1,0:T(8,128)(2,1)} %bitcast.5, s32[1,768]{1,0:T(1,128)} %sends.1, s32[3,128]{1,0:T(4,128)} %bitcast.7, bf16[128,3,128,128]{3,2,1,0:T(8,128)(2,1)} %w.1, f32[27,16,128]{2,1,0:T(8,128)} %bitcast.6, f32[9,16,128]{2,1,0:T(8,128)} %mass_in.1, ...), custom_call_target="tpu_custom_call" | custom-call | tf_op jit(solution)/shard_map/remap_and_steps/pallas_call | solution.py:590
  68.9 1.0 %copy.12 = f32[19,8,16,128]{3,2,1,0:T(8,128)} copy(f32[19,8,16,128]{3,2,1,0:T(8,128)S(1)} %get-tuple-element.8) | data formatting | bytes 2490368
  70.0 0.7 copy.13

commit v4 on v3

--- a/solution.py
+++ b/solution.py
@@ -21,6 +21,7 @@
 ORDERS = (("x", "y", "z"), ("y", "z", "x"), ("z", "x", "y"))
 CHUNKS = ((0, 4, 0), (4, 3, 1), (7, 3, 2), (10, 3, 0), (13, 3, 1), (16, 3, 2))
 WAVES = ((0, 1, 2), (3, 4, 5))
+PIECES = len(CHUNKS)
 SPOTS = 36
 NODES = 27
 
@@ -33,7 +34,7 @@
     old, sends, asks_in, w, vel_in, mass_in, spot_x_in, spot_y_in,
     state_out, v_out, *scratch,
 ):
-    hbuf, sbuf, ubuf, gbuf = (scratch[n * 6:n * 6 + 6] for n in range(4))
+    hbuf, sbuf, ubuf, gbuf = (scratch[n * PIECES:(n + 1) * PIECES] for n in range(4))
     (
         sbuf_in, spread, psel, qsel, xs, wv, rem,
         vext, vcol, dtm, dtmc, press, pressc, ddx, ddy, dsm, s6, fm, cl, cr,
@@ -43,20 +44,20 @@
         asks, vel, mass, spot_x, spot_y, st, vout,
         p1_s, p1_r, ix_s, ix_r, p2_s, p2_r, p3_s, p3_r, loc1, locx, loc2, loc3, wsem,
         hs, hr, e1_s, e1_r, e2_s, e2_r, load, out_sem,
-    ) = scratch[24:]
+    ) = scratch[4 * PIECES:]
     di = lax.axis_index("gx")
     dj = lax.axis_index("gy")
-    here = {"z": di // 2, "c": di % 2, "y": dj // 4, "x": dj % 4}
+    here = {"z": lax.div(di, 2), "c": lax.rem(di, 2), "y": lax.div(dj, 4), "x": lax.rem(dj, 4)}
 
     def device(**moved):
         at = dict(here)
         for axis, step in moved.items():
             size = 2 if axis == "c" else 4
-            at[axis] = (at[axis] + step) % size
+            at[axis] = lax.rem(at[axis] + step, size)
         return (at["z"] * 2 + at["c"], at["y"] * 4 + at["x"])
 
     def plate(a, b):
-        return ((di + a + 8) % 8, (dj + b + 16) % 16)
+        return (lax.rem(di + (a + 8), 8), lax.rem(dj + (b + 16), 16))
 
     around = [(a, b) for a in (-1, 0, 1) for b in (-1, 0, 1) if (a, b) != (0, 0)]
     partners = [device(**{axis: d, "c": c}) for axis in "xyz" for d in (1, 2, 3) for c in (0, 1)]
@@ -87,7 +88,7 @@
         copy.start()
     pl.semaphore_wait(barrier, len(partners))
 
-    phase1, onward = {}, {}
+    phase1 = {}
 
     def start_phase1(wave):
         for q in wave:
@@ -97,23 +98,11 @@
                 remote(
                     old.at[pl.ds(first, count)], hbuf[q].at[here[ga]], p1_s.at[q, n], p1_r.at[q, n], device(**{ga: d})
                 )
-                for n, d in enumerate((1, 3))
+                for n, d in enumerate((1, 3, 2))
             ]
-        for n in (0, 1):
+        for n in range(len(phase1[q])):
             for q in wave:
                 phase1[q][n].start()
-
-    def start_onward(wave):
-        for q in wave:
-            first, count, order = CHUNKS[q]
-            ga = ORDERS[order][0]
-            half = count // 2 if q % 2 == 0 else count - count // 2
-            onward[q] = []
-            for n, (d, back, part) in enumerate(((1, 3, pl.ds(0, half)), (3, 1, pl.ds(half, count - half)))):
-                phase1[q][n].wait_recv()
-                held = hbuf[q].at[(here[ga] + back) % 4, part]
-                onward[q].append(remote(held, held, p1_s.at[q, 2 + n], p1_r.at[q, 2 + n], device(**{ga: d})))
-                onward[q][n].start()
 
     lists = []
     for d in (1, 2, 3):
@@ -122,8 +111,8 @@
                 sends, sbuf_in.at[o, here[ga]], ix_s.at[o, d - 1], ix_r.at[o, d - 1], device(**{ga: d})
             )))
             lists[-1][1].start()
-    start_phase1(WAVES[0])
-    start_phase1(WAVES[1])
+    for wave in WAVES:
+        start_phase1(wave)
 
     weights = [
         pltpu.make_async_copy(w.at[pl.ds(n * 32, 32)], wv.at[pl.ds(n * 32, 32)], wsem.at[n]) for n in range(4)
@@ -155,16 +144,21 @@
         copy.start()
 
     t192, c768 = iota((192, 128), 0), iota((192, 128), 1)
-    aim, part = t192 // 6, t192 % 6
-    on_p, on_q, on_c = aim // 8, (aim // 2) % 4, aim % 2
+    aim = (t192 * 10923) >> 16
+    part = t192 - aim * 6
+    on_p, on_q, on_c = aim >> 3, (aim >> 1) & 3, aim & 1
     for o, (ga, pa, qa) in enumerate(ORDERS):
         at = {ga: here[ga], pa: on_p, qa: on_q}
         stands = (((at["z"] * 2 + on_c) * 4 + at["y"]) * 4 + at["x"]) * 6 + part
         for m in range(6):
             spread[o, :, m * 128:(m + 1) * 128] = jnp.where(stands == c768 + m * 128, 1.0, 0.0).astype(BF16)
-    r768 = iota((768, 256), 0)
-    widen = jnp.where((r768 // 24) * 6 + r768 % 6 == iota((768, 256), 1), 1.0, 0.0).astype(BF16)
-    source_of = (iota((768, 128), 0) // 6) % 4
+    r768 = iota((768, 128), 0)
+    sixes = (r768 * 10923) >> 16
+    source_of = sixes & 3
+    short_row = (sixes >> 2) * 6 + r768 - sixes * 6
+    widen = jnp.concatenate(
+        [jnp.where(short_row == iota((768, 128), 1) + m, 1.0, 0.0).astype(BF16) for m in (0, 128)], axis=1
+    )
     lanes768 = iota((768, 128), 1).astype(F32)
 
     phase2 = {}
@@ -186,7 +180,7 @@
 
     def arrived(q):
         local1[q].wait()
-        for copy in onward[q]:
+        for copy in phase1[q]:
             copy.wait_recv()
 
     def start_phase2(q):
@@ -201,7 +195,7 @@
         own = pltpu.make_async_copy(sbuf[q].at[mine], ubuf[q].at[mine], loc2.at[q])
         own.start()
         copies = [
-            remote(sbuf[q].at[(mine + d) % 4], ubuf[q].at[mine], p2_s.at[q, d - 1], p2_r.at[q, d - 1], device(**{pa: d}))
+            remote(sbuf[q].at[lax.rem(mine + d, 4)], ubuf[q].at[mine], p2_s.at[q, d - 1], p2_r.at[q, d - 1], device(**{pa: d}))
             for d in (2, 1, 3)
         ]
         for copy in copies:
@@ -224,7 +218,7 @@
         for d in (2, 1, 3, 0):
             for c in (0, 1):
                 if (d, c) != (0, 0):
-                    there = ((here[qa] + d) % 4) * 2 + (here["c"] + c) % 2
+                    there = lax.rem(here[qa] + d, 4) * 2 + lax.rem(here["c"] + c, 2)
                     slot = d * 2 + c - 1
                     copies.append(remote(
                         ubuf[q].at[:, there], gbuf[q].at[mine], p3_s.at[q, slot], p3_r.at[q, slot], device(**{qa: d, "c": c})
@@ -252,11 +246,8 @@
         for n in range(count):
             xs[pl.ds(first + n, 384, stride=24), :] = picked[:, n * 128:(n + 1) * 128]
 
-    selection(0)
-    start_onward(WAVES[0])
-    selection(1)
-    selection(2)
-    start_onward(WAVES[1])
+    for o in range(3):
+        selection(o)
     for q in WAVES[0]:
         arrived(q)
         start_phase2(q)
@@ -295,9 +286,10 @@
     press[...] = -PEAK_PRESSURE * main
     pressc[...] = jnp.where(lane24 == NODES - 1, -PEAK_PRESSURE * side, 0.0)
 
-    for q in WAVES[1]:
-        arrived(q)
-        start_phase2(q)
+    for wave in WAVES[1:]:
+        for q in wave:
+            arrived(q)
+            start_phase2(q)
     for copy in weights:
         copy.wait()
     for q in WAVES[0]:
@@ -506,8 +498,8 @@
     v_copy.start()
     for o, copy in lists:
         copy.wait_send()
-    for q in range(6):
-        for copy in phase1[q] + onward[q] + phase2[q][1] + phase3[q][1]:
+    for q in range(PIECES):
+        for copy in phase1[q] + phase2[q][1] + phase3[q][1]:
             copy.wait_send()
     for copy in halo + round1 + round2:
         copy.wait_send()
@@ -582,7 +574,7 @@
         + [
             pltpu.SemaphoreType.DMA(shape)
             for shape in (
-                (6, 4), (6, 4), (3, 3), (3, 3), (6, 3), (6, 3), (6, 7), (6, 7), (6,), (3,), (6,), (6,), (4,),
+                (6, 3), (6, 3), (3, 3), (3, 3), (6, 3), (6, 3), (6, 7), (6, 7), (6,), (3,), (6,), (6,), (4,),
                 (3,), (3,), (8,), (8,), (3,), (3,), (5,), (2,),
             )
         ]

time: 70.8 us -> 70.5 us (level)
  no operation moved by 1% of the time
where the time goes in v4:
time: 70.5 us; the launch traced here: 70 us
  Pallas kernels  67.6 us (96%)
  local copies, waits for them, and re-layouts  1.72 us (2%)
    pallas_call x1, Pallas kernels, body(): pl.pallas_call(kernel, out_shape=(jax.ShapeDtypeStruct((19, 8, 16, 128),...  67.6 us
    unnamed x2, local copies, waits for them, and re-layouts  1.72 us

profile of v4, /device:TPU:1, one launch (start us, length us, event | category | flops | bytes accessed | tf_op | source)
XLA Modules:
  0.0 70.0 jit_solution(7627970252282470231)
XLA Ops:
  0.6 67.6 %remap_and_steps.1 = (f32[19,8,16,128]{3,2,1,0:T(8,128)S(1)}, f32[27,16,128]{2,1,0:T(8,128)S(1)}) custom-call(bf16[19,128,128]{2,1,0:T(8,128)(2,1)} %bitcast.5, s32[1,768]{1,0:T(1,128)} %sends.1, s32[3,128]{1,0:T(4,128)} %bitcast.7, bf16[128,3,128,128]{3,2,1,0:T(8,128)(2,1)} %w.1, f32[27,16,128]{2,1,0:T(8,128)} %bitcast.6, f32[9,16,128]{2,1,0:T(8,128)} %mass_in.1, ...), custom_call_target="tpu_custom_call" | custom-call | tf_op jit(solution)/shard_map/remap_and_steps/pallas_call | solution.py:582
  68.3 1.0 %copy.12 = f32[19,8,16,128]{3,2,1,0:T(8,128)} copy(f32[19,8,16,128]{3,2,1,0:T(8,128)S(1)} %get-tuple-element.8) | data formatting | bytes 2490368
  69.3 0.7 copy.13

commit v5 on v4

--- a/solution.py
+++ b/solution.py
@@ -19,7 +19,7 @@
 BF16 = jnp.bfloat16
 
 ORDERS = (("x", "y", "z"), ("y", "z", "x"), ("z", "x", "y"))
-CHUNKS = ((0, 4, 0), (4, 3, 1), (7, 3, 2), (10, 3, 0), (13, 3, 1), (16, 3, 2))
+CHUNKS = ((0, 4, 0), (4, 4, 1), (8, 4, 2), (12, 3, 0), (15, 2, 1), (17, 2, 2))
 WAVES = ((0, 1, 2), (3, 4, 5))
 PIECES = len(CHUNKS)
 SPOTS = 36
@@ -316,10 +316,13 @@
     used = (lane24 < NODES) & (row24 < 17)
     dtmc[...] = jnp.where(used, high_j * row_mask * TIME_STEP / jnp.where(used, heavy, 1.0), 0.0)
 
-    def differences():
+    def differences(left_force=None):
         edge = lane24 == 127
         for n in range(NODES):
             v = vext[n]
+            if left_force is not None:
+                v = v + jnp.where(lane24 == 0, left_force[:, n:n + 1], 0.0) * dtm[n % 9]
+                vext[n] = v
             right = jnp.where(edge, vcol[:, n:n + 1], pltpu.roll(v, 127, 1))
             total = v + right
             delta = right - v
@@ -449,7 +452,17 @@
     )
     for copy in round1:
         copy.start()
-    for copy in round1:
+    for copy in round1[6:]:
+        copy.wait_recv()
+    for n in range(NODES):
+        rows = jnp.concatenate([
+            jnp.where(first8, row_up_in[n:n + 1] * low_i, 0.0), zeros8, jnp.where(first8, row_dn_in[n:n + 1] * high_i, 0.0)
+        ], axis=0)
+        force = fm[n] + rows
+        if n == NODES - 1:
+            force = force + press[...]
+        vext[n] = vext[n] + force * dtm[n % 9]
+    for copy in round1[:6]:
         copy.wait_recv()
 
     def ends(at_low, at_high):
@@ -461,16 +474,7 @@
     add_right = high_j * (cl_in[...] + ends(diag_in[2], diag_in[3]))
     col_force = cr[...] + add_right + ends(row_up_in[32:40], row_dn_in[32:40]) + pressc[...]
     vcol[...] = vcol[...] + col_force * dtmc[...]
-    for n in range(NODES):
-        rows = jnp.concatenate([
-            jnp.where(first8, row_up_in[n:n + 1] * low_i, 0.0), zeros8, jnp.where(first8, row_dn_in[n:n + 1] * high_i, 0.0)
-        ], axis=0)
-        force = fm[n] + rows + jnp.where(lane24 == 0, add_left[:, n:n + 1], 0.0)
-        if n == NODES - 1:
-            force = force + press[...]
-        vext[n] = vext[n] + force * dtm[n % 9]
-
-    differences()
+    differences(add_left)
     elements(1)
     left, right = forces(True)
     cr2[...] = right

time: 70.5 us -> 70.7 us (level)
  no operation moved by 1% of the time
where the time goes in v5:
time: 70.7 us; the launch traced here: 70.2 us
  Pallas kernels  67.9 us (96%)
  local copies, waits for them, and re-layouts  1.72 us (2%)
    pallas_call x1, Pallas kernels, body(): pl.pallas_call(kernel, out_shape=(jax.ShapeDtypeStruct((19, 8, 16, 128),...  67.9 us
    unnamed x2, local copies, waits for them, and re-layouts  1.72 us

profile of v5, /device:TPU:1, one launch (start us, length us, event | category | flops | bytes accessed | tf_op | source)
XLA Modules:
  0.0 70.2 jit_solution(14631777023581781749)
XLA Ops:
  0.6 67.9 %remap_and_steps.1 = (f32[19,8,16,128]{3,2,1,0:T(8,128)S(1)}, f32[27,16,128]{2,1,0:T(8,128)S(1)}) custom-call(bf16[19,128,128]{2,1,0:T(8,128)(2,1)} %bitcast.5, s32[1,768]{1,0:T(1,128)} %sends.1, s32[3,128]{1,0:T(4,128)} %bitcast.7, bf16[128,3,128,128]{3,2,1,0:T(8,128)(2,1)} %w.1, f32[27,16,128]{2,1,0:T(8,128)} %bitcast.6, f32[9,16,128]{2,1,0:T(8,128)} %mass_in.1, ...), custom_call_target="tpu_custom_call" | custom-call | tf_op jit(solution)/shard_map/remap_and_steps/pallas_call | solution.py:586
  68.5 1.0 %copy.12 = f32[19,8,16,128]{3,2,1,0:T(8,128)} copy(f32[19,8,16,128]{3,2,1,0:T(8,128)S(1)} %get-tuple-element.8) | data formatting | bytes 2490368
  69.5 0.7 copy.13
